TPU v7x, 512 devices: a whole 4x4x16 slice. The times are simulated.
512 devices in a mesh: dp: 32 (over z_lo, y, core), rows: 16 (over x, z_hi).
Axes of the slice: x: 4, y: 4, z: 16 (z_hi: 4, z_lo: 4; z = z_hi * 4 + z_lo), core: 2. Of those that a mesh axis runs over, the one named last changes fastest.
Arguments:
- fine_level: bfloat16 [32, 192, 48, 384], P('dp', 'rows'), may hold values from -6 to 6
- coarse_level: bfloat16 [32, 96, 24, 384], P('dp', 'rows'), may hold values from -6 to 6
- merging_weights: float32 [2], replicated, may hold values from 0.3 to 3
- depth_weight: float32 [3, 3, 384], replicated, may hold values from -2 to 2
- point_weight: bfloat16 [384, 384], replicated, may hold values from -0.3125 to 0.3125
- norm_gain: float32 [384], replicated, may hold values from 0.5 to 1.5
- cotangent: bfloat16 [32, 192, 48, 384], P('dp', 'rows'), may hold values from -48 to 48
Outputs:
- grad_fine: bfloat16 [32, 192, 48, 384], P('dp', 'rows')
- grad_coarse: bfloat16 [32, 96, 24, 384], P('dp', 'rows')
- grad_merging: float32 [2], replicated
- grad_depth: float32 [3, 3, 384], replicated
- grad_point: bfloat16 [384, 384], replicated
- grad_gain: float32 [384], replicated
- grad_shift: float32 [384], replicated
All inputs are finite; a program needn't handle non-finite values.
Results may differ from a plain program's by a relative error of at most 0.02.
Values may be sent and summed in bfloat16 or wider, within the bound.
No kernel may reach another device: no remote copies, remote signals or barrier semaphores. Data moves between devices by JAX's collectives and lax.ppermute only.
A program may use at most 64 MiB of HBM per device.

v0:
```python
import jax
import jax.numpy as jnp
from jax import lax
from jax.sharding import PartitionSpec as P


def padded_2(cells, sides, width):
    for axis, dim in sides:
        count = lax.axis_size(axis)
        ends = count - 1
        head = lax.slice_in_dim(cells, 0, width, axis=dim)
        tail = lax.slice_in_dim(cells, cells.shape[dim] - width, cells.shape[dim], axis=dim)
        cells = jnp.concatenate(
            [
                lax.ppermute(tail, axis, [(i, (i + 1) % count) for i in range(ends)]),
                cells,
                lax.ppermute(head, axis, [((i + 1) % count, i) for i in range(ends)]),
            ],
            axis=dim,
        )
    return cells


def pad_columns(field):
    return jnp.pad(field, ((0, 0), (0, 0), (1, 1), (0, 0)))


def depthwise(extended, depth_weight, height):
    padded = pad_columns(extended).astype(jnp.float32)
    width = extended.shape[2]
    result = jnp.zeros((extended.shape[0], height, width, extended.shape[3]), jnp.float32)
    for a in range(3):
        for b in range(3):
            result = result + padded[:, a : a + height, b : b + width] * depth_weight[a, b]
    return result


def on_device(
    fine_level, coarse_level, merging_weights, depth_weight, point_weight, norm_gain, cotangent
):
    height, width, channels = (fine_level.shape[1], fine_level.shape[2], fine_level.shape[3])
    total = merging_weights[0] + merging_weights[1] + 0.0001
    upsampled = jnp.repeat(jnp.repeat(coarse_level, 2, axis=1), 2, axis=2).astype(jnp.float32)
    fine_float = fine_level.astype(jnp.float32)
    merged = (merging_weights[0] * fine_float + merging_weights[1] * upsampled) / total
    sig = jax.nn.sigmoid(merged)
    activated = (merged * sig).astype(jnp.bfloat16)
    count = lax.axis_size("dp") * lax.axis_size("rows") * height * width
    act_rim = padded_2(activated, (("rows", 1),), 1)
    depth_ext = depthwise(act_rim, depth_weight, height).astype(jnp.bfloat16)
    projected_ext = jnp.einsum(
        "nhwc,cd->nhwd", depth_ext, point_weight, preferred_element_type=jnp.float32
    )
    grad_out = cotangent.astype(jnp.float32)
    sums, squares = lax.psum(
        (
            jnp.sum(projected_ext, axis=(0, 1, 2)),
            jnp.sum(projected_ext * projected_ext, axis=(0, 1, 2)),
        ),
        ("dp", "rows"),
    )
    mean = sums / count
    variance = squares / count - mean * mean
    inv_std = 1.0 / jnp.sqrt(variance + 1e-05)
    normed = (projected_ext - mean) * inv_std
    grad_shift, grad_gain = lax.psum(
        (jnp.sum(grad_out, axis=(0, 1, 2)), jnp.sum(grad_out * normed, axis=(0, 1, 2))),
        ("dp", "rows"),
    )
    scale_term = norm_gain * inv_std
    grad_proj = (scale_term * (grad_out - grad_shift / count - normed * grad_gain / count)).astype(
        jnp.bfloat16
    )
    grad_map = jnp.einsum(
        "nhwd,cd->nhwc", grad_proj, point_weight, preferred_element_type=jnp.float32
    ).astype(jnp.bfloat16)
    grad_map_ext = padded_2(grad_map, (("rows", 1),), 1)
    point_part = jnp.einsum(
        "nhwc,nhwd->cd", depth_ext, grad_proj, preferred_element_type=jnp.float32
    )
    act_padded = pad_columns(act_rim).astype(jnp.float32)
    grad_map_float = grad_map.astype(jnp.float32)
    depth_part = jnp.stack(
        [
            jnp.sum(act_padded[:, a : a + height, b : b + width] * grad_map_float, axis=(0, 1, 2))
            for a in range(3)
            for b in range(3)
        ]
    )
    grad_padded = pad_columns(grad_map_ext).astype(jnp.float32)
    grad_act = jnp.zeros(fine_level.shape, jnp.float32)
    for a in range(3):
        for b in range(3):
            grad_act = (
                grad_act
                + grad_padded[:, 2 - a : 2 - a + height, 2 - b : 2 - b + width] * depth_weight[a, b]
            )
    grad_merged = grad_act * sig * (1.0 + merged * (1.0 - sig))
    grad_fine = (grad_merged * merging_weights[0] / total).astype(jnp.bfloat16)
    blocks = grad_merged.reshape(1, height // 2, 2, width // 2, 2, channels).sum(axis=(2, 4))
    grad_coarse = (blocks * merging_weights[1] / total).astype(jnp.bfloat16)
    merging_part = jnp.stack(
        [
            jnp.sum(grad_merged * (fine_float - merged) / total, axis=(0, 1, 2)),
            jnp.sum(grad_merged * (upsampled - merged) / total, axis=(0, 1, 2)),
        ]
    )
    stacked = jnp.concatenate([point_part, depth_part, merging_part], axis=0)
    summed = lax.psum(stacked, ("dp", "rows"))
    grad_point = summed[:channels].astype(jnp.bfloat16)
    grad_depth = summed[channels : channels + 9].reshape(3, 3, channels)
    grad_merging = jnp.sum(summed[channels + 9 :], axis=1)
    return (grad_fine, grad_coarse, grad_merging, grad_depth, grad_point, grad_gain, grad_shift)


def solution(mesh):
    placed = (
        P("dp", "rows", None, None),
        P("dp", "rows", None, None),
        P(),
        P(),
        P(),
        P(),
        P("dp", "rows", None, None),
    )
    return jax.shard_map(
        on_device,
        mesh=mesh,
        in_specs=placed,
        out_specs=(
            P("dp", "rows", None, None),
            P("dp", "rows", None, None),
            P(),
            P(),
            P(),
            P(),
            P(),
        ),
        check_vma=False,
    )
```

profile of v0, /device:TPU:1, one launch (start us, length us, event | category | flops | bytes accessed | tf_op | source)
XLA Modules:
  0.0 729.7 jit_solution(15344015422437605436)
XLA Ops:
  7.2 1.3 fusion.50
  8.5 0.9 bitcast_convert_fusion
  9.5 0.3 broadcast_in_dim.5
  9.8 0.6 convert_element_type.84
  11.8 1.6 multiply_convert_fusion
  13.4 9.6 %collective-permute-start = (bf16[1,1,48,384]{3,2,1,0:T(8,128)(2,1)S(1)}, bf16[1,1,48,384]{3,2,1,0:T(8,128)(2,1)S(1)}, u32[]{:S(2)}, u32[]{:S(2)}) collective-permute-start(bf16[1,1,48,384]{3,2,1,0:T(8,128)(2,1)S(1)} %get-tuple-element.38), channel_id=1, source_target_pairs={{0,1},{1,2},{2,3},{3,4},{4,5},{5,6},{6,7},{7,8},{8,9},{9,10},{10,1... | collective-permute-start | bytes 110600 | tf_op jit(solution)/shard_map/ppermute | solution.py:15
  23.1 1.3 collective-permute-start.1
  24.4 8.8 %collective-permute-done.1 = bf16[1,1,48,384]{3,2,1,0:T(8,128)(2,1)S(1)} collective-permute-done((bf16[1,1,48,384]{3,2,1,0:T(8,128)(2,1)S(1)}, bf16[1,1,48,384]{3,2,1,0:T(8,128)(2,1)S(1)}, u32[]{:S(2)}, u32[]{:S(2)}) %collective-permute-start.1) | collective-permute-done | bytes 36896 | tf_op jit(solution)/shard_map/ppermute | solution.py:17
  33.4 0.6 add_convert_fusion
  34.0 0.8 copy-done.3
  34.8 0.5 fusion.46
  35.2 104.4 %all-reduce.3 = (f32[384]{0:T(512)S(1)}, f32[384]{0:T(512)S(1)}) all-reduce(f32[384]{0:T(512)S(1)} %get-tuple-element.19, f32[384]{0:T(512)S(1)} %get-tuple-element.18), channel_id=1, replica_groups=mesh['dp'=32,'rows'=16] {'dp','rows'}, use_global_device_ids=true, to_apply=%region_1.2 | all-reduce | flops 768 | bytes 6144 | tf_op jit(solution)/shard_map/psum | solution.py:55
  139.7 1.2 convert_reduce_fusion
  140.9 99.7 %all-reduce.2 = (f32[384]{0:T(512)S(1)}, f32[384]{0:T(512)S(1)}) all-reduce(f32[384]{0:T(512)S(1)} %get-tuple-element.21, f32[384]{0:T(512)S(1)} %get-tuple-element.20), channel_id=1, replica_groups=mesh['dp'=32,'rows'=16] {'dp','rows'}, use_global_device_ids=true, to_apply=%region_7.8 | all-reduce | flops 768 | bytes 6144 | tf_op jit(solution)/shard_map/psum | solution.py:66
  240.6 1.3 fusion.38
  241.9 1.2 fusion.18
  243.2 5.3 collective-permute-start.2
  248.5 1.3 collective-permute-start.3
  249.8 0.5 convolution_bitcast_fusion
  250.4 6.8 collective-permute-done.3
  257.2 0.1 fusion.31
  257.4 2.6 fusion.29
  260.0 2.6 concatenate.11
  262.6 0.5 reshape.142
  263.2 0.6 reduce_sum.157
  263.8 1.3 fusion.44
  265.1 1.5 divide_convert_fusion
  266.6 451.8 %all-reduce.6.cloned.1.call-done = f32[395,384]{1,0:T(8,128)} async-done(((f32[395,384]{1,0:T(8,128)}), f32[395,384]{1,0:T(8,128)}) %all-reduce.6.cloned.1.call-update) | async-done | bytes 606736 | tf_op jit(solution)/shard_map/psum | solution.py:109
  718.4 0.7 slice.190
  719.1 0.6 reshape.143
  719.7 1.3 slice_reduce_fusion
  721.1 1.8 slice.266
  (39 shorter events, 0.4 us)
Async XLA Ops:
  7.2 27.6 %copy-start = (bf16[384,384]{1,0:T(8,128)(2,1)S(1)}, bf16[384,384]{1,0:T(8,128)(2,1)}, u32[]{:S(2)}) copy-start(bf16[384,384]{1,0:T(8,128)(2,1)} %param.11) | copy-start | bytes 884740
  7.2 711.2 %all-reduce.6.cloned.1.call-start = ((), (), s32[]{:S(2)}) async-start(), calls=%async_computation | async-start | bytes 1228800 | tf_op jit(solution)/shard_map/psum | solution.py:109
  9.8 2.0 copy-start.1
  10.4 13.9 %copy-start.5 = (f32[3,3,384]{2,1,0:T(4,128)S(1)}, f32[3,3,384]{2,1,0:T(4,128)}, u32[]{:S(2)}) copy-start(f32[3,3,384]{2,1,0:T(4,128)} %param.10) | copy-start | bytes 41476
  13.4 11.0 %collective-permute-start = (bf16[1,1,48,384]{3,2,1,0:T(8,128)(2,1)S(1)}, bf16[1,1,48,384]{3,2,1,0:T(8,128)(2,1)S(1)}, u32[]{:S(2)}, u32[]{:S(2)}) collective-permute-start(bf16[1,1,48,384]{3,2,1,0:T(8,128)(2,1)S(1)} %get-tuple-element.38), channel_id=1, source_target_pairs={{0,1},{1,2},{2,3},{3,4},{4,5},{5,6},{6,7},{7,8},{8,9},{9,10},{10,1... | collective-permute-start | bytes 110600 | tf_op jit(solution)/shard_map/ppermute | solution.py:15
  23.1 10.2 %collective-permute-start.1 = (bf16[1,1,48,384]{3,2,1,0:T(8,128)(2,1)S(1)}, bf16[1,1,48,384]{3,2,1,0:T(8,128)(2,1)S(1)}, u32[]{:S(2)}, u32[]{:S(2)}) collective-permute-start(bf16[1,1,48,384]{3,2,1,0:T(8,128)(2,1)S(1)} %get-tuple-element.39), channel_id=1, source_target_pairs={{1,0},{2,1},{3,2},{4,3},{5,4},{6,5},{7,6},{8,7},{9,8},{10,9},{11,1... | collective-permute-start | bytes 110600 | tf_op jit(solution)/shard_map/ppermute | solution.py:17
  34.0 0.8 copy-start.3
  34.8 104.9 %copy-start.7 = (f32[384]{0:T(512)S(1)}, f32[384]{0:T(512)}, u32[]{:S(2)}) copy-start(f32[384]{0:T(512)} %param.12) | copy-start | bytes 4612
  240.6 2.6 copy-start.6
  240.6 2.6 copy-start.8
  241.9 7.9 %copy-start.4 = (bf16[1,12,48,384]{3,2,1,0:T(8,128)(2,1)S(1)}, bf16[1,12,48,384]{3,2,1,0:T(8,128)(2,1)}, u32[]{:S(2)}) copy-start(bf16[1,12,48,384]{3,2,1,0:T(8,128)(2,1)} %copy-done.3) | copy-start | bytes 1327108
  243.2 7.2 collective-permute-start.2
  248.5 8.7 %collective-permute-start.3 = (bf16[1,1,48,384]{3,2,1,0:T(8,128)(2,1)S(1)}, bf16[1,1,48,384]{3,2,1,0:T(8,128)(2,1)S(1)}, u32[]{:S(2)}, u32[]{:S(2)}) collective-permute-start(bf16[1,1,48,384]{3,2,1,0:T(8,128)(2,1)S(1)} %get-tuple-element.37), channel_id=1, source_target_pairs={{1,0},{2,1},{3,2},{4,3},{5,4},{6,5},{7,6},{8,7},{9,8},{10,9},{11,1... | collective-permute-start | bytes 110600 | tf_op jit(solution)/shard_map/ppermute | solution.py:17
  250.3 7.1 copy-start.2
Sparse Core Ops, SparseCore 0:
  262.8 455.5 all-reduce.5
where the time goes:
time: 730 us
  waiting for transfers between devices  467 us (64%)
  blocking collectives  204 us (28%)
  starting transfers between devices  17.5 us (2%)
  between operations  15.7 us (2%)
  other arithmetic  13.3 us (2%)
  local copies, waits for them, and re-layouts  9.51 us (1%)
    psum x1, waiting for transfers between devices, on_device(): summed = lax.psum(stacked, ('dp', 'rows'))  452 us
    psum x1, blocking collectives, on_device(): lax.psum((jnp.sum(projected_ext, axis=(0, 1, 2)), jnp.sum(projected_ext *...  104 us
    psum x1, blocking collectives, on_device(): lax.psum((jnp.sum(grad_out, axis=(0, 1, 2)), jnp.sum(grad_out * normed, a...  99.7 us
    ppermute x2, waiting for transfers between devices, padded_2(): lax.ppermute(head, axis, [((i + 1) % count, i) for i in range(ends)])  15.6 us
    ppermute x2, starting transfers between devices, padded_2(): lax.ppermute(tail, axis, [(i, (i + 1) % count) for i in range(ends)])  14.9 us
  transfers between devices with their start and end apart: 5, of which 3 were waited for; matrix products, arithmetic and copies ran while one was open for 1% of the time, Pallas kernels for 0%

commit v1 on v0

v1 whole, which is shorter than its diff:
```python
import jax
import jax.numpy as jnp
from jax import lax
from jax.sharding import PartitionSpec as P

AXES = ("dp", "rows")
COUNT = 294912
bf16, f32 = jnp.bfloat16, jnp.float32


def groups_of(bits):
    rest = [b for b in range(9) if b not in bits]

    def spread(value, places):
        return sum(((value >> i) & 1) << b for i, b in enumerate(places))

    return [
        [spread(r, rest) + spread(m, bits) for m in range(1 << len(bits))]
        for r in range(1 << len(rest))
    ]


PLANE = groups_of([2, 3, 4, 5, 6])
DEPTH = groups_of([0, 1, 7, 8])


def exchange(parts, groups):
    return lax.all_to_all(parts, AXES, 0, 0, axis_index_groups=groups)


def spread_to(block, groups):
    return exchange(jnp.broadcast_to(block[None], (len(groups[0]),) + block.shape), groups)


def summed_over(block, groups):
    return jnp.sum(spread_to(block, groups), axis=0)


def two_parts(values):
    high = values.astype(bf16)
    return high, (values - high.astype(f32)).astype(bf16)


def pad_columns(field):
    return jnp.pad(field, ((0, 0), (1, 1), (0, 0)))


def on_device(
    fine_level, coarse_level, merging_weights, depth_weight, point_weight, norm_gain, cotangent
):
    fine, coarse, cot = fine_level[0], coarse_level[0], cotangent[0]
    height, width, channels = fine.shape
    half = width // 2

    def pack(fine_rows, coarse_row, cot_row):
        return jnp.concatenate([fine_rows.reshape(-1, channels), coarse_row, cot_row], axis=0)

    head = pack(fine[:2], coarse[0], cot[0])
    tail = pack(fine[-2:], coarse[-1], cot[-1])
    n = lax.axis_size("rows")
    above = lax.ppermute(tail, "rows", [(i, i + 1) for i in range(n - 1)])
    below = lax.ppermute(head, "rows", [(i + 1, i) for i in range(n - 1)])

    def unpack(packed):
        return (
            packed[: 2 * width].reshape(2, width, channels),
            packed[2 * width : 2 * width + half][None],
            packed[2 * width + half :][None],
        )

    fa, ca, ga = unpack(above)
    fb, cb, gb = unpack(below)
    fine_ext = jnp.concatenate([fa, fine, fb], axis=0).astype(f32)
    coarse_ext = jnp.concatenate([ca, coarse, cb], axis=0)
    cot_ext = jnp.concatenate([ga, cot, gb], axis=0).astype(f32)

    total = merging_weights[0] + merging_weights[1] + 0.0001
    up_ext = jnp.repeat(jnp.repeat(coarse_ext, 2, axis=0), 2, axis=1).astype(f32)
    merged_ext = (merging_weights[0] * fine_ext + merging_weights[1] * up_ext) / total
    sig_ext = jax.nn.sigmoid(merged_ext)
    act = pad_columns((merged_ext * sig_ext).astype(bf16)).astype(f32)
    rows = height + 2
    depth = jnp.zeros((rows, width, channels), f32)
    for a in range(3):
        for b in range(3):
            depth = depth + act[a : a + rows, b : b + width] * depth_weight[a, b]
    depth = depth.astype(bf16)
    projected = jnp.einsum("hwc,cd->hwd", depth, point_weight, preferred_element_type=f32)
    own = projected[1:-1]
    own_cot = cot_ext[1:-1]
    stats = jnp.stack(
        [
            jnp.sum(own, axis=(0, 1)),
            jnp.sum(own * own, axis=(0, 1)),
            jnp.sum(own_cot, axis=(0, 1)),
            jnp.sum(own_cot * own, axis=(0, 1)),
        ]
    )
    stats = summed_over(summed_over(stats.reshape(12, 128), PLANE), DEPTH).reshape(4, channels)
    mean = stats[0] / COUNT
    variance = stats[1] / COUNT - mean * mean
    inv_std = 1.0 / jnp.sqrt(variance + 1e-05)
    grad_shift = stats[2]
    grad_gain = inv_std * (stats[3] - mean * grad_shift)

    normed = (projected - mean) * inv_std
    grad_proj = (
        norm_gain * inv_std * (cot_ext - grad_shift / COUNT - normed * grad_gain / COUNT)
    ).astype(bf16)
    point_part = jnp.einsum(
        "hwc,hwd->cd", depth[1:-1], grad_proj[1:-1], preferred_element_type=f32
    )
    grad_map = jnp.einsum("hwd,cd->hwc", grad_proj, point_weight, preferred_element_type=f32)
    place = lax.axis_index("rows")
    row = jnp.arange(rows).reshape(rows, 1, 1)
    outside = ((place == 0) & (row == 0)) | ((place == n - 1) & (row == rows - 1))
    grad_map = jnp.where(outside, 0.0, grad_map).astype(bf16).astype(f32)
    own_map = grad_map[1:-1]
    depth_part = jnp.stack(
        [
            jnp.sum(act[a + 1 : a + 1 + height, b : b + width] * own_map, axis=(0, 1))
            for a in range(3)
            for b in range(3)
        ]
    )
    padded = pad_columns(grad_map)
    grad_act = jnp.zeros((height, width, channels), f32)
    for a in range(3):
        for b in range(3):
            grad_act = (
                grad_act + padded[2 - a : 2 - a + height, 2 - b : 2 - b + width] * depth_weight[a, b]
            )
    merged, sig, fine_float, up = (
        merged_ext[2:-2],
        sig_ext[2:-2],
        fine_ext[2:-2],
        up_ext[2:-2],
    )
    grad_merged = grad_act * sig * (1.0 + merged * (1.0 - sig))
    grad_fine = (grad_merged * merging_weights[0] / total).astype(bf16)
    blocks = grad_merged.reshape(height // 2, 2, half, 2, channels).sum(axis=(1, 3))
    grad_coarse = (blocks * merging_weights[1] / total).astype(bf16)
    merging_part = jnp.stack(
        [
            jnp.sum(grad_merged * (fine_float - merged) / total, axis=(0, 1)),
            jnp.sum(grad_merged * (up - merged) / total, axis=(0, 1)),
        ]
    )
    small = jnp.concatenate([depth_part, merging_part], axis=0).reshape(32, -1)
    many = small.shape[1]

    def joined(point, rest):
        return jnp.concatenate([point.astype(bf16), *two_parts(rest)], axis=-1)

    def parted(both):
        both = both.astype(f32)
        return both[..., : -2 * many], both[..., -2 * many : -many] + both[..., -many:]

    point, rest = parted(exchange(joined(point_part.reshape(32, -1), small), PLANE))
    point, rest = jnp.sum(point, axis=0), jnp.sum(rest, axis=0)
    point, rest = parted(spread_to(joined(point, rest), DEPTH))
    point, rest = jnp.sum(point, axis=0), jnp.sum(rest, axis=0)
    point, rest = parted(spread_to(joined(point, rest), PLANE))
    grad_point = point.astype(bf16).reshape(channels, channels)
    rest = rest.reshape(11, channels)
    grad_depth = rest[:9].reshape(3, 3, channels)
    grad_merging = jnp.sum(rest[9:], axis=1)
    return (
        grad_fine[None],
        grad_coarse[None],
        grad_merging,
        grad_depth,
        grad_point,
        grad_gain,
        grad_shift,
    )


def solution(mesh):
    split = P("dp", "rows", None, None)
    return jax.shard_map(
        on_device,
        mesh=mesh,
        in_specs=(split, split, P(), P(), P(), P(), split),
        out_specs=(split, split, P(), P(), P(), P(), P()),
        check_vma=False,
    )
```

time: 730 us -> 151 us (0.21)
  waiting for transfers between devices: 467 us -> 33.9 us
  blocking collectives: 204 us -> 15.5 us
  starting transfers between devices: 17.5 us -> 50.7 us
  local copies, waits for them, and re-layouts: 9.51 us -> 23.8 us
  between operations: 15.7 us -> 2.84 us
  other arithmetic: 13.3 us -> 20.7 us
    psum x1 -> x0, waiting for transfers between devices: 452 us -> none  [on_device(): summed = lax.psum(stacked, ('dp', 'rows'))]
    psum x2 -> x0, blocking collectives: 204 us -> none  [the longest x1 104 us: on_device(): lax.psum((jnp.sum(projected_ext, axis=(0, 1, 2)), jnp.sum(projected_ext *...]
    all_to_all x0 -> x4, starting transfers between devices: none -> 39.2 us  [exchange(): return lax.all_to_all(parts, AXES, 0, 0, axis_index_groups=groups)]
    all_to_all x0 -> x4, waiting for transfers between devices: none -> 33.9 us  [exchange(): return lax.all_to_all(parts, AXES, 0, 0, axis_index_groups=groups)]
    ppermute x4 -> x2, waiting for transfers between devices: 15.6 us -> 0.01 us  [the longest x1 0.01 us: on_device(): above = lax.ppermute(tail, 'rows', [(i, i + 1) for i in range(n - 1)])]
    all_to_all x0 -> x1, blocking collectives: none -> 15.5 us  [exchange(): return lax.all_to_all(parts, AXES, 0, 0, axis_index_groups=groups)]
    ppermute x4 -> x2, starting transfers between devices: 17.5 us -> 11.6 us  [the longest x1 10.3 us: on_device(): above = lax.ppermute(tail, 'rows', [(i, i + 1) for i in range(n - 1)])]
  transfers between devices with their start and end apart: 5 -> 6, of which waited for: 3 -> 4; matrix products, arithmetic and copies ran while one was open for 1% -> 9% of each run, Pallas kernels for 0% -> 0%
where the time goes in v1:
time: 151 us; the launch traced here: 150 us
  starting transfers between devices  50.7 us (34%)
  waiting for transfers between devices  33.9 us (22%)
  local copies, waits for them, and re-layouts  23.8 us (16%)
  other arithmetic  20.7 us (14%)
  blocking collectives  15.5 us (10%)
  between operations  2.84 us (2%)
  matrix products  2.14 us (1%)
    all_to_all x4, starting transfers between devices, exchange(): return lax.all_to_all(parts, AXES, 0, 0, axis_index_groups=groups)  39.2 us
    all_to_all x4, waiting for transfers between devices, exchange(): return lax.all_to_all(parts, AXES, 0, 0, axis_index_groups=groups)  33.9 us
    all_to_all x1, blocking collectives, exchange(): return lax.all_to_all(parts, AXES, 0, 0, axis_index_groups=groups)  15.5 us
    ppermute x1, starting transfers between devices, on_device(): above = lax.ppermute(tail, 'rows', [(i, i + 1) for i in range(n - 1)])  10.3 us
    unnamed x92, local copies, waits for them, and re-layouts  6.71 us
    broadcast_in_dim x2, other arithmetic, spread_to(): jnp.broadcast_to(block[None], (len(groups[0]),) + block.shape)  4.22 us
  transfers between devices with their start and end apart: 6, of which 4 were waited for; matrix products, arithmetic and copies ran while one was open for 9% of the time, Pallas kernels for 0%

profile of v1, /device:TPU:1, one launch (start us, length us, event | category | flops | bytes accessed | tf_op | source)
XLA Modules:
  0.0 149.6 jit_solution(3027185473244534364)
XLA Ops:
  0.7 1.0 fusion.60
  3.2 1.3 collective-permute-start.1
  4.6 10.3 %collective-permute-start = (bf16[168,384]{1,0:T(8,128)(2,1)S(1)}, bf16[168,384]{1,0:T(8,128)(2,1)S(1)}, u32[]{:S(2)}, u32[]{:S(2)}) collective-permute-start(bf16[168,384]{1,0:T(8,128)(2,1)S(1)} %pad_maximum_fusion), channel_id=1, source_target_pairs={{0,1},{1,2},{2,3},{3,4},{4,5},{5,6},{6,7},{7,8},{8,9},{9,10},{10,1... | collective-permute-start | bytes 387080 | tf_op jit(solution)/shard_map/ppermute | solution.py:61
  14.8 1.3 fusion.61
  17.4 1.5 %slice_reduce_fusion.13 = (f32[384]{0:T(512)}, f32[384]{0:T(512)}, f32[384]{0:T(512)}, f32[384]{0:T(512)}, f32[384]{0:T(512)}, /*index=5*/f32[384]{0:T(512)}, f32[384]{0:T(512)}, f32[384]{0:T(512)}, f32[384]{0:T(512)}) fusion(f32[3,3,384]{2,1,0:T(4,128)} %param.10), kind=kLoop, calls=%fused_computation.135 | loop fusion | bytes 27648 | tf_op jit(solution)/shard_map/slice | solution.py:86
  20.8 0.8 mul.309
  21.8 2.0 %add_divide_fusion = (f32[16,48,384]{2,1,0:T(8,128)}, f32[16,48,384]{2,1,0:T(8,128)S(1)}) fusion(f32[]{:T(128)S(6)} %add.91, f32[16,48,384]{2,1,0:T(8,128)S(1)} %mul.309, bf16[2,48,384]{2,1,0:T(8,128)(2,1)S(1)} %bitcast.92, bf16[12,48,384]{2,1,0:T(8,128)(2,1)S(1)} %bitcast.81, bf16[2,48,384]{2,1,0:T(8,128)(2,1)S(1)} %bitcast.90, f32[]{:T(128)} %bitcast), kind=kLoop, calls=%fused_computation.12 | loop fusion | flops 2654208 | bytes 4128776 | tf_op jit(solution)/shard_map/div | solution.py:80
  27.9 24.1 %all-to-all-start = ((f32[32,12,128]{2,1,0:T(8,128)}), f32[32,12,128]{2,1,0:T(8,128)S(1)}, u32[]{:S(2)}, u32[]{:S(2)}) async-start(f32[32,12,128]{2,1,0:T(8,128)} %broadcast_in_dim.77), calls=%async_computation | async-start | bytes 524288 | tf_op jit(solution)/shard_map/all_to_all | solution.py:28
  52.0 8.9 %all-to-all-done = f32[32,12,128]{2,1,0:T(8,128)S(1)} async-done(((f32[32,12,128]{2,1,0:T(8,128)}), f32[32,12,128]{2,1,0:T(8,128)S(1)}, u32[]{:S(2)}, u32[]{:S(2)}) %all-to-all-start) | async-done | bytes 196640 | tf_op jit(solution)/shard_map/all_to_all | solution.py:28
  61.5 1.4 broadcast_in_dim.78
  62.9 4.5 %all-to-all-start.1 = ((f32[16,12,128]{2,1,0:T(8,128)}), f32[16,12,128]{2,1,0:T(8,128)}, u32[]{:S(2)}, u32[]{:S(2)}) async-start(f32[16,12,128]{2,1,0:T(8,128)} %broadcast_in_dim.78), calls=%async_computation.1 | async-start | bytes 262144 | tf_op jit(solution)/shard_map/all_to_all | solution.py:28
  67.4 0.9 maximum_convert_fusion.2
  68.5 1.3 broadcast_in_dim.81
  69.7 2.7 %slice.318 = f32[12,48,384]{2,1,0:T(8,128)} reshape(f32[12,24,2,384]{3,2,1,0:T(2,128)} %broadcast_in_dim.81) | data formatting | bytes 1769472 | tf_op jit(solution)/shard_map/slice | solution.py:137
  72.5 1.1 maximum_convert_fusion
  73.7 6.4 %all-to-all-done.1 = f32[16,12,128]{2,1,0:T(8,128)} async-done(((f32[16,12,128]{2,1,0:T(8,128)}), f32[16,12,128]{2,1,0:T(8,128)}, u32[]{:S(2)}, u32[]{:S(2)}) %all-to-all-start.1) | async-done | bytes 98336 | tf_op jit(solution)/shard_map/all_to_all | solution.py:28
  80.1 0.9 reduce_sum.212
  81.1 1.6 %multiply_convert_fusion.1 = bf16[14,48,384]{2,1,0:T(8,128)(2,1)S(1)} fusion(f32[14,48,384]{2,1,0:T(8,128)} %copy-done.1, f32[384]{0:T(512)S(1)} %fusion.50, f32[384]{0:T(512)S(1)} %get-tuple-element.53, f32[384]{0:T(512)S(1)} %fusion.51, f32[384]{0:T(512)S(1)} %get-tuple-element.44, f32[384]{0:T(512)S(1)} %get-tuple-element.52, ...), kind=kLoop, calls=%fused_computation.32 | loop fusion | flops 2838528 | bytes 2072064 | tf_op jit(solution)/shard_map/convert_element_type | solution.py:109
  82.7 1.2 fusion.2
  86.4 1.0 fusion.39
  89.8 15.5 %all_to_all.31 = bf16[32,2,2436]{2,1,0:T(2,128)(2,1)S(1)} all-to-all(bf16[32,2,2436]{2,1,0:T(2,128)(2,1)S(1)} %reshape.196), channel_id=1, replica_groups={{0,4,8,12,16,20,24,28,32,36,40,44,48,52,56,60,64,68,72,76,80,84,88,92,9..., dimensions={0} | all-to-all | bytes 623616 | tf_op jit(solution)/shard_map/all_to_all | solution.py:28
  106.3 1.6 %reduce.19 = bf16[16,4872]{1,0:T(8,128)(2,1)S(1)} reduce(bf16[16,1,4872]{2,1,0:T(2,128)(2,1)S(1)} %broadcast_in_dim.82, bf16[]{:T(256)} %broadcast.144), dimensions={1}, to_apply=%broadcast_in_dim.82.reduce_sub_computation | reduce | bytes 311810 | tf_op jit(solution)/shard_map/broadcast_in_dim | solution.py:32
  107.9 0.9 reshape.198
  108.8 3.7 %all-to-all-start.3 = ((bf16[16,2,2436]{2,1,0:T(2,128)(2,1)}), bf16[16,2,2436]{2,1,0:T(2,128)(2,1)S(1)}, u32[]{:S(2)}, u32[]{:S(2)}) async-start(bf16[16,2,2436]{2,1,0:T(2,128)(2,1)} %reshape.198), calls=%async_computation.3 | async-start | bytes 327680 | tf_op jit(solution)/shard_map/all_to_all | solution.py:28
  113.6 11.8 %all-to-all-done.3 = bf16[16,2,2436]{2,1,0:T(2,128)(2,1)S(1)} async-done(((bf16[16,2,2436]{2,1,0:T(2,128)(2,1)}), bf16[16,2,2436]{2,1,0:T(2,128)(2,1)S(1)}, u32[]{:S(2)}, u32[]{:S(2)}) %all-to-all-start.3) | async-done | bytes 155936 | tf_op jit(solution)/shard_map/all_to_all | solution.py:28
  126.2 2.6 %reduce.20 = bf16[32,4872]{1,0:T(8,128)(2,1)S(1)} reduce(bf16[32,1,4872]{2,1,0:T(2,128)(2,1)S(1)} %broadcast_in_dim.83, bf16[]{:T(256)} %broadcast.144), dimensions={1}, to_apply=%broadcast_in_dim.83.reduce_sub_computation | reduce | bytes 623618 | tf_op jit(solution)/shard_map/broadcast_in_dim | solution.py:32
  128.9 1.1 reshape.200
  130.0 6.9 %all-to-all-start.4 = ((bf16[32,2,2436]{2,1,0:T(2,128)(2,1)}), bf16[32,2,2436]{2,1,0:T(2,128)(2,1)S(1)}, u32[]{:S(2)}, u32[]{:S(2)}) async-start(bf16[32,2,2436]{2,1,0:T(2,128)(2,1)} %reshape.200), calls=%async_computation.4 | async-start | bytes 655360 | tf_op jit(solution)/shard_map/all_to_all | solution.py:28
  136.9 1.3 fusion.46
  138.2 1.5 fusion.42
  139.7 6.8 %all-to-all-done.4 = bf16[32,2,2436]{2,1,0:T(2,128)(2,1)S(1)} async-done(((bf16[32,2,2436]{2,1,0:T(2,128)(2,1)}), bf16[32,2,2436]{2,1,0:T(2,128)(2,1)S(1)}, u32[]{:S(2)}, u32[]{:S(2)}) %all-to-all-start.4) | async-done | bytes 311840 | tf_op jit(solution)/shard_map/all_to_all | solution.py:28
  147.1 1.1 reshape.182
  (163 shorter events, 17.7 us)
Async XLA Ops:
  0.6 24.9 %copy-start = (bf16[384,384]{1,0:T(8,128)(2,1)S(1)}, bf16[384,384]{1,0:T(8,128)(2,1)}, u32[]{:S(2)}) copy-start(bf16[384,384]{1,0:T(8,128)(2,1)} %param.11) | copy-start | bytes 884740
  0.6 18.9 %copy-start.13 = (bf16[1,6,24,384]{3,2,1,0:T(8,128)(2,1)S(1)}, bf16[1,6,24,384]{3,2,1,0:T(8,128)(2,1)}, u32[]{:S(2)}) copy-start(bf16[1,6,24,384]{3,2,1,0:T(8,128)(2,1)} %param.8) | copy-start | bytes 331780
  3.2 15.7 %collective-permute-start.1 = (bf16[168,384]{1,0:T(8,128)(2,1)S(1)}, bf16[168,384]{1,0:T(8,128)(2,1)S(1)}, u32[]{:S(2)}, u32[]{:S(2)}) collective-permute-start(bf16[168,384]{1,0:T(8,128)(2,1)S(1)} %pad_maximum_fusion.1), channel_id=1, source_target_pairs={{1,0},{2,1},{3,2},{4,3},{5,4},{6,5},{7,6},{8,7},{9,8},{10,9},{11,1... | collective-permute-start | bytes 387080 | tf_op jit(solution)/shard_map/ppermute | solution.py:62
  4.6 14.4 %collective-permute-start = (bf16[168,384]{1,0:T(8,128)(2,1)S(1)}, bf16[168,384]{1,0:T(8,128)(2,1)S(1)}, u32[]{:S(2)}, u32[]{:S(2)}) collective-permute-start(bf16[168,384]{1,0:T(8,128)(2,1)S(1)} %pad_maximum_fusion), channel_id=1, source_target_pairs={{0,1},{1,2},{2,3},{3,4},{4,5},{5,6},{6,7},{7,8},{8,9},{9,10},{10,1... | collective-permute-start | bytes 387080 | tf_op jit(solution)/shard_map/ppermute | solution.py:61
  21.6 2.1 %copy-start.9 = (bf16[96,384]{1,0:T(8,128)(2,1)}, bf16[96,384]{1,0:T(8,128)(2,1)S(1)}, u32[]{:S(2)}) copy-start(bf16[96,384]{1,0:T(8,128)(2,1)S(1)} %slice.330) | copy-start | bytes 221188
  21.6 2.1 %copy-start.11 = (bf16[96,384]{1,0:T(8,128)(2,1)}, bf16[96,384]{1,0:T(8,128)(2,1)S(1)}, u32[]{:S(2)}) copy-start(bf16[96,384]{1,0:T(8,128)(2,1)S(1)} %slice.331) | copy-start | bytes 221188
  25.6 1.3 copy-start.7
  27.9 33.0 %all-to-all-start = ((f32[32,12,128]{2,1,0:T(8,128)}), f32[32,12,128]{2,1,0:T(8,128)S(1)}, u32[]{:S(2)}, u32[]{:S(2)}) async-start(f32[32,12,128]{2,1,0:T(8,128)} %broadcast_in_dim.77), calls=%async_computation | async-start | bytes 524288 | tf_op jit(solution)/shard_map/all_to_all | solution.py:28
  62.9 17.2 %all-to-all-start.1 = ((f32[16,12,128]{2,1,0:T(8,128)}), f32[16,12,128]{2,1,0:T(8,128)}, u32[]{:S(2)}, u32[]{:S(2)}) async-start(f32[16,12,128]{2,1,0:T(8,128)} %broadcast_in_dim.78), calls=%async_computation.1 | async-start | bytes 262144 | tf_op jit(solution)/shard_map/all_to_all | solution.py:28
  69.7 2.7 %copy-start.10 = (bf16[96,384]{1,0:T(8,128)(2,1)S(1)}, bf16[96,384]{1,0:T(8,128)(2,1)}, u32[]{:S(2)}) copy-start(bf16[96,384]{1,0:T(8,128)(2,1)} %copy-done.9) | copy-start | bytes 221188
  69.7 2.7 %copy-start.12 = (bf16[96,384]{1,0:T(8,128)(2,1)S(1)}, bf16[96,384]{1,0:T(8,128)(2,1)}, u32[]{:S(2)}) copy-start(bf16[96,384]{1,0:T(8,128)(2,1)} %copy-done.11) | copy-start | bytes 221188
  72.5 8.5 %copy-start.41 = (f32[384]{0:T(512)S(1)}, f32[384]{0:T(512)}, u32[]{:S(2)}) copy-start(f32[384]{0:T(512)} %param.12) | copy-start | bytes 4612
  72.5 8.6 %copy-start.15 = (bf16[1,48,384]{2,1,0:T(8,128)(2,1)S(1)}, bf16[1,48,384]{2,1,0:T(8,128)(2,1)}, u32[]{:S(2)}) copy-start(bf16[1,48,384]{2,1,0:T(8,128)(2,1)} %copy-done.14) | copy-start | bytes 110596
  72.5 8.6 %copy-start.17 = (bf16[1,48,384]{2,1,0:T(8,128)(2,1)S(1)}, bf16[1,48,384]{2,1,0:T(8,128)(2,1)}, u32[]{:S(2)}) copy-start(bf16[1,48,384]{2,1,0:T(8,128)(2,1)} %copy-done.16) | copy-start | bytes 110596
  73.7 9.1 %copy-start.8 = (bf16[14,48,384]{2,1,0:T(8,128)(2,1)S(1)}, bf16[14,48,384]{2,1,0:T(8,128)(2,1)}, u32[]{:S(2)}) copy-start(bf16[14,48,384]{2,1,0:T(8,128)(2,1)} %copy-done.7) | copy-start | bytes 1548292
  81.0 2.9 %copy-start.40 = (f32[384]{0:T(512)}, f32[384]{0:T(512)S(1)}, u32[]{:S(2)}) copy-start(f32[384]{0:T(512)S(1)} %get-tuple-element.45) | copy-start | bytes 4612
  81.1 2.9 %copy-start.39 = (f32[384]{0:T(512)}, f32[384]{0:T(512)S(1)}, u32[]{:S(2)}) copy-start(f32[384]{0:T(512)S(1)} %fusion.50) | copy-start | bytes 4612
  84.4 1.3 copy-start.2
  84.4 1.6 %copy-start.3 = (f32[16,48,384]{2,1,0:T(8,128)S(1)}, f32[16,48,384]{2,1,0:T(8,128)}, u32[]{:S(2)}) copy-start(f32[16,48,384]{2,1,0:T(8,128)} %maximum_convert_fusion) | copy-start | bytes 3538948
  84.4 1.9 %copy-start.4 = (f32[12,48,384]{2,1,0:T(8,128)S(1)}, f32[12,48,384]{2,1,0:T(8,128)}, u32[]{:S(2)}) copy-start(f32[12,48,384]{2,1,0:T(8,128)} %slice.318) | copy-start | bytes 2654212
  84.4 1.9 %copy-start.22 = (f32[384]{0:T(512)S(1)}, f32[384]{0:T(512)}, u32[]{:S(2)}) copy-start(f32[384]{0:T(512)} %get-tuple-element.22) | copy-start | bytes 4612
  84.5 1.8 %copy-start.24 = (f32[384]{0:T(512)S(1)}, f32[384]{0:T(512)}, u32[]{:S(2)}) copy-start(f32[384]{0:T(512)} %get-tuple-element.23) | copy-start | bytes 4612
  84.5 1.8 %copy-start.26 = (f32[384]{0:T(512)S(1)}, f32[384]{0:T(512)}, u32[]{:S(2)}) copy-start(f32[384]{0:T(512)} %get-tuple-element.24) | copy-start | bytes 4612
  84.5 1.8 %copy-start.28 = (f32[384]{0:T(512)S(1)}, f32[384]{0:T(512)}, u32[]{:S(2)}) copy-start(f32[384]{0:T(512)} %get-tuple-element.25) | copy-start | bytes 4612
  84.5 1.8 %copy-start.30 = (f32[384]{0:T(512)S(1)}, f32[384]{0:T(512)}, u32[]{:S(2)}) copy-start(f32[384]{0:T(512)} %get-tuple-element.26) | copy-start | bytes 4612
  84.5 1.8 %copy-start.32 = (f32[384]{0:T(512)S(1)}, f32[384]{0:T(512)}, u32[]{:S(2)}) copy-start(f32[384]{0:T(512)} %get-tuple-element.27) | copy-start | bytes 4612
  84.5 1.8 %copy-start.34 = (f32[384]{0:T(512)S(1)}, f32[384]{0:T(512)}, u32[]{:S(2)}) copy-start(f32[384]{0:T(512)} %get-tuple-element.28) | copy-start | bytes 4612
  84.5 1.8 %copy-start.36 = (f32[384]{0:T(512)S(1)}, f32[384]{0:T(512)}, u32[]{:S(2)}) copy-start(f32[384]{0:T(512)} %get-tuple-element.29) | copy-start | bytes 4612
  84.5 1.8 %copy-start.38 = (f32[384]{0:T(512)S(1)}, f32[384]{0:T(512)}, u32[]{:S(2)}) copy-start(f32[384]{0:T(512)} %get-tuple-element.30) | copy-start | bytes 4612
  86.4 1.3 copy-start.18
  108.8 16.6 %all-to-all-start.3 = ((bf16[16,2,2436]{2,1,0:T(2,128)(2,1)}), bf16[16,2,2436]{2,1,0:T(2,128)(2,1)S(1)}, u32[]{:S(2)}, u32[]{:S(2)}) async-start(bf16[16,2,2436]{2,1,0:T(2,128)(2,1)} %reshape.198), calls=%async_computation.3 | async-start | bytes 327680 | tf_op jit(solution)/shard_map/all_to_all | solution.py:28
  130.0 16.5 %all-to-all-start.4 = ((bf16[32,2,2436]{2,1,0:T(2,128)(2,1)}), bf16[32,2,2436]{2,1,0:T(2,128)(2,1)S(1)}, u32[]{:S(2)}, u32[]{:S(2)}) async-start(bf16[32,2,2436]{2,1,0:T(2,128)(2,1)} %reshape.200), calls=%async_computation.4 | async-start | bytes 655360 | tf_op jit(solution)/shard_map/all_to_all | solution.py:28
  (16 other events, 11.9 us)

commit v2 on v1

v2 whole, which is shorter than its diff:
```python
import jax
import jax.numpy as jnp
from jax import lax
from jax.experimental import pallas as pl
from jax.experimental.pallas import tpu as pltpu
from jax.sharding import PartitionSpec as P

AXES = ("dp", "rows")
COUNT = 294912
HEIGHT, WIDTH, CH, LANES = 12, 48, 384, 128
HALF = WIDTH // 2
MID = HEIGHT - 2
PIECE = 36
SLOT = 40
bf16, f32 = jnp.bfloat16, jnp.float32


def groups_of(bits):
    rest = [b for b in range(9) if b not in bits]

    def spread(value, places):
        return sum(((value >> i) & 1) << b for i, b in enumerate(places))

    return [
        [spread(r, rest) + spread(m, bits) for m in range(1 << len(bits))]
        for r in range(1 << len(rest))
    ]


PLANE = groups_of([2, 3, 4, 5, 6])
DEPTH = groups_of([0, 1, 7, 8])


def exchange(parts, groups):
    return lax.all_to_all(parts, AXES, 0, 0, axis_index_groups=groups)


def column():
    return lax.broadcasted_iota(jnp.int32, (WIDTH, LANES), 0)


def from_left(x):
    return jnp.where(column() == 0, 0.0, pltpu.roll(x, 1, 0))


def from_right(x):
    return jnp.where(column() == WIDTH - 1, 0.0, pltpu.roll(x, WIDTH - 1, 0))


def shares(weights):
    first, second = jnp.full((1, LANES), weights[0]), jnp.full((1, LANES), weights[1])
    total = first + second + 0.0001
    return first / total, second / total, total


def doubled(coarse):
    n = coarse.shape[0]
    row = lax.broadcasted_iota(jnp.int32, (2 * n, n), 0)
    place = lax.broadcasted_iota(jnp.int32, (2 * n, n), 1)
    pick = jnp.where((row == 2 * place) | (row == 2 * place + 1), 1.0, 0.0).astype(bf16)
    return jnp.dot(pick, coarse, preferred_element_type=f32)


def blocks():
    return [slice(c * LANES, (c + 1) * LANES) for c in range(CH // LANES)]


def activate(fine, up, share):
    merged = share[0] * fine + share[1] * up
    sig = jax.nn.sigmoid(merged)
    return merged, sig, (merged * sig).astype(bf16).astype(f32)


def convolve(act, i, dw, c):
    rows = [act[i + a - 1, :, c] for a in range(3)]
    across = [sum(rows[a] * dw[a, b : b + 1, c] for a in range(3)) for b in range(3)]
    return from_left(across[0]) + across[1] + from_right(across[2])


def folded(x):
    return jnp.sum(x.reshape(-1, 8, x.shape[-1]), axis=0)


def statistics(proj, cot):
    parts = (proj, proj * proj, cot, cot * proj)
    return [jnp.sum(folded(p), axis=0, keepdims=True) for p in parts]


def pack_kernel(ft, fb, ct, cb, gt, gb, head, tail):
    n = 2 * WIDTH
    for out, fine, coarse, cot in ((head, ft, ct, gt), (tail, fb, cb, gb)):
        out[0:WIDTH] = fine[0, 0]
        out[WIDTH:n] = fine[0, 1]
        out[n : n + WIDTH] = cot[0, 0]
        out[n + WIDTH : n + WIDTH + HALF] = coarse[0, 0]


def middle_kernel(mw, fine, coarse, dw, pw, cot, depth, proj, stats, act, up):
    share = shares(mw)
    up[...] = doubled(coarse[0].reshape(-1, CH))
    for c in blocks():
        for i in range(HEIGHT):
            u = up[(i // 2) * WIDTH : (i // 2 + 1) * WIDTH, c]
            act[i, :, c] = activate(fine[0, i, :, c].astype(f32), u, share)[2]
        for i in range(1, HEIGHT - 1):
            depth[(i - 1) * WIDTH : i * WIDTH, c] = convolve(act, i, dw, c).astype(bf16)
    proj[...] = jnp.dot(depth[...], pw[...], preferred_element_type=f32)
    own = cot[0, 1 : HEIGHT - 1].reshape(-1, CH).astype(f32)
    for k, s in enumerate(statistics(proj[...], own)):
        stats[k : k + 1] = s


def edge_kernel(mw, above, below, ft, fb, ct, cb, gt, gb, dw, pw, mid, depth, proj, stats, act):
    share = shares(mw)
    n = 2 * WIDTH
    for e in range(2):
        halo, fine, coarse = (above, ft, ct) if e == 0 else (below, fb, cb)
        far = doubled(halo[n + WIDTH : n + WIDTH + HALF])
        near = doubled(coarse[0, 0])
        for c in blocks():
            for r in range(2):
                h, o = (r, r + 2) if e == 0 else (r + 2, r)
                outer = halo[r * WIDTH : (r + 1) * WIDTH, c].astype(f32)
                act[e, h, :, c] = activate(outer, far[:, c], share)[2]
                act[e, o, :, c] = activate(fine[0, r, :, c].astype(f32), near[:, c], share)[2]
            for r in range(2):
                at = (2 * e + r) * WIDTH
                depth[at : at + WIDTH, c] = convolve(act.at[e], r + 1, dw, c).astype(bf16)
    proj[...] = jnp.dot(depth[...], pw[...], preferred_element_type=f32)
    first = statistics(proj[WIDTH : 2 * WIDTH], gt[0, 0].astype(f32))
    last = statistics(proj[2 * WIDTH : 3 * WIDTH], gb[0, 0].astype(f32))
    whole = jnp.concatenate([x + y for x, y in zip(first, last)], axis=0) + mid[...]
    stats[...] = jnp.broadcast_to(whole[None], stats.shape)


def total_kernel(parts, out):
    out[...] = jnp.broadcast_to(jnp.sum(parts[...], axis=0)[None], out.shape)


def backward_kernel(
    mw, gathered, above, below, fine, coarse, dw, pw, gain, cot, depth_mid, depth_edge,
    proj_mid, proj_edge, grad_fine, grad_coarse, send, grad_gain, grad_shift,
    own_depth, gproj, gmap, up, pairs, point, slots,
):
    share = shares(mw)
    n = 2 * WIDTH
    stats = jnp.sum(gathered[...], axis=0)
    mean = stats[0:1] / COUNT
    variance = stats[1:2] / COUNT - mean * mean
    inv_std = 1.0 / jnp.sqrt(variance + 1e-05)
    shift = stats[2:3]
    gained = inv_std * (stats[3:4] - mean * shift)
    grad_gain[...] = gained
    grad_shift[...] = shift
    scale = gain[...] * inv_std
    by_proj = -(scale * inv_std * gained) / COUNT
    offset = -(scale * shift) / COUNT

    def gradient(g, p):
        return (scale * g.astype(f32) + (by_proj * (p - mean) + offset)).astype(bf16)

    end = HEIGHT * WIDTH
    gproj[0:WIDTH] = gradient(above[n : n + WIDTH], proj_edge[0:WIDTH])
    gproj[WIDTH:n] = gradient(cot[0, 0], proj_edge[WIDTH:n])
    mid_cot = cot[0, 1 : HEIGHT - 1].reshape(-1, CH)
    gproj[n : end] = gradient(mid_cot, proj_mid[...])
    gproj[end : end + WIDTH] = gradient(cot[0, HEIGHT - 1], proj_edge[n : n + WIDTH])
    gproj[end + WIDTH : end + n] = gradient(below[n : n + WIDTH], proj_edge[n + WIDTH : 2 * n])
    own_depth[0:WIDTH] = depth_edge[WIDTH:n]
    own_depth[WIDTH : end - WIDTH] = depth_mid[...]
    own_depth[end - WIDTH : end] = depth_edge[n : n + WIDTH]
    at_place = lax.axis_index("rows")
    keep = (
        jnp.where(at_place == 0, 0.0, 1.0),
        jnp.where(at_place == lax.axis_size("rows") - 1, 0.0, 1.0),
    )
    whole_map = lax.dot_general(
        gproj[...], pw[...], (((1,), (1,)), ((), ())), preferred_element_type=f32
    ).astype(bf16).astype(f32)
    whole_point = lax.dot_general(
        own_depth[...], gproj[WIDTH : end + WIDTH], (((0,), (0,)), ((), ())),
        preferred_element_type=f32,
    )
    for k, c in enumerate(blocks()):
        point[k * CH : (k + 1) * CH] = whole_point[:, c]
        for r in range(HEIGHT + 2):
            x = whole_map[r * WIDTH : (r + 1) * WIDTH, c]
            if r == 0:
                x = x * keep[0]
            if r == HEIGHT + 1:
                x = x * keep[1]
            gmap[0, r, :, c] = from_right(x)
            gmap[1, r, :, c] = x
            gmap[2, r, :, c] = from_left(x)
    up[...] = doubled(coarse[0].reshape(-1, CH))
    by_weight = [jnp.zeros((8, LANES), f32)] * 2
    zero = jnp.zeros((1, LANES), f32)
    small = [zero] * 32
    for k, c in enumerate(blocks()):
        taps = [jnp.zeros((8, LANES), f32)] * 9
        for p in range(HEIGHT):
            fine_row = fine[0, p, :, c].astype(f32)
            u = up[(p // 2) * WIDTH : (p // 2 + 1) * WIDTH, c]
            merged, sig, act = activate(fine_row, u, share)
            grad_act = jnp.zeros((WIDTH, LANES), f32)
            for a in range(3):
                for b in range(3):
                    x = gmap[b, p + 2 - a, :, c]
                    grad_act = grad_act + x * dw[a, b : b + 1, c]
                    taps[3 * a + b] = taps[3 * a + b] + folded(act * x)
            grad_merged = grad_act * (sig * (1.0 + merged * (1.0 - sig)))
            grad_fine[0, p, :, c] = (grad_merged * share[0]).astype(bf16)
            by_weight[0] = by_weight[0] + folded(grad_merged * (fine_row - merged))
            by_weight[1] = by_weight[1] + folded(grad_merged * (u - merged))
            at = k * HEIGHT * HALF + (p // 2) * WIDTH
            if p % 2 == 0:
                pairs[at : at + WIDTH] = grad_merged
            else:
                pairs[at : at + WIDTH] = pairs[at : at + WIDTH] + grad_merged
        for t in range(9):
            small[3 * t + k] = jnp.sum(taps[t], axis=0, keepdims=True)
    for t in range(2):
        small[27 + t] = jnp.sum(by_weight[t], axis=0, keepdims=True) / share[2]
    m = HEIGHT * HALF // 2
    for k, c in enumerate(blocks()):
        both = pairs[pl.ds(2 * k * m, m, stride=2)] + pairs[pl.ds(2 * k * m + 1, m, stride=2)]
        grad_coarse[0, :, :, c] = (both * share[1]).astype(bf16).reshape(HEIGHT // 2, HALF, LANES)
    for s in range(32):
        slots[s, 0:PIECE] = point[s * PIECE : (s + 1) * PIECE]
        high = small[s].astype(bf16).astype(f32)
        slots[s, PIECE:SLOT] = jnp.concatenate([high, small[s] - high, zero, zero], axis=0)
    send[...] = slots[...].astype(bf16)


def relay_kernel(parts, out):
    total = jnp.sum(parts[...].astype(f32), axis=0)
    value = total[PIECE : PIECE + 1] + total[PIECE + 1 : PIECE + 2]
    high = value.astype(bf16).astype(f32)
    row = lax.broadcasted_iota(jnp.int32, (SLOT, LANES), 0)
    total = jnp.where(row == PIECE, high, jnp.where(row == PIECE + 1, value - high, total))
    out[...] = jnp.broadcast_to(total.astype(bf16)[None], out.shape)


def finish_kernel(parts, grad_point, grad_depth, grad_merging, point):
    rest = []
    for s in range(32):
        slot = parts[s].astype(f32)
        point[s * PIECE : (s + 1) * PIECE] = slot[0:PIECE]
        rest.append(slot[PIECE : PIECE + 1] + slot[PIECE + 1 : PIECE + 2])
    for k, c in enumerate(blocks()):
        grad_point[:, c] = point[k * CH : (k + 1) * CH].astype(bf16)
        for t in range(9):
            grad_depth[t // 3, t % 3 : t % 3 + 1, c] = rest[3 * t + k]
    sums = [jnp.sum(rest[27 + t], axis=1, keepdims=True) for t in range(2)]
    grad_merging[...] = jnp.concatenate(sums, axis=1)


VMEM = pl.BlockSpec(memory_space=pltpu.VMEM)
SMEM = pl.BlockSpec(memory_space=pltpu.SMEM)


def call(kernel, name, outs, scratch=(), in_specs=None, cost=0, grid=()):
    return pl.pallas_call(
        kernel,
        name=name,
        grid=grid,
        out_shape=[jax.ShapeDtypeStruct(s, t) for s, t in outs],
        in_specs=in_specs or [VMEM],
        out_specs=[VMEM] * len(outs),
        scratch_shapes=[pltpu.VMEM(s, t) for s, t in scratch],
        compiler_params=pltpu.CompilerParams(vmem_limit_bytes=32 * 1024 * 1024),
        cost_estimate=pl.CostEstimate(flops=cost, bytes_accessed=1 << 20, transcendentals=0),
    )


def edge_specs():
    def at(shape, row):
        return pl.BlockSpec(shape, lambda i: (0, row, 0, 0))

    fine, coarse, cot = (1, 2, WIDTH, CH), (1, 1, HALF, CH), (1, 1, WIDTH, CH)
    return [
        at(fine, 0), at(fine, HEIGHT // 2 - 1), at(coarse, 0), at(coarse, HEIGHT // 2 - 1),
        at(cot, 0), at(cot, HEIGHT - 1),
    ]


def on_device(
    fine_level, coarse_level, merging_weights, depth_weight, point_weight, norm_gain, cotangent
):
    ends = (fine_level, fine_level, coarse_level, coarse_level, cotangent, cotangent)
    packed = (3 * WIDTH + HALF, CH)
    head, tail = call(pack_kernel, "pack", [(packed, bf16)] * 2, in_specs=edge_specs(), grid=(1,))(
        *ends
    )
    n = lax.axis_size("rows")
    above = lax.ppermute(tail, "rows", [(i, i + 1) for i in range(n - 1)])
    below = lax.ppermute(head, "rows", [(i + 1, i) for i in range(n - 1)])
    depth_mid, proj_mid, mid = call(
        middle_kernel,
        "middle",
        [((MID * WIDTH, CH), bf16), ((MID * WIDTH, CH), f32), ((4, CH), f32)],
        [((HEIGHT, WIDTH, CH), f32), ((HEIGHT * HALF, CH), f32)],
        [SMEM] + [VMEM] * 5,
        cost=1 << 28,
    )(merging_weights, fine_level, coarse_level, depth_weight, point_weight, cotangent)
    depth_edge, proj_edge, stats = call(
        edge_kernel,
        "edge",
        [((4 * WIDTH, CH), bf16), ((4 * WIDTH, CH), f32), ((32, 4, CH), f32)],
        [((2, 4, WIDTH, CH), f32)],
        [SMEM, VMEM, VMEM] + edge_specs() + [VMEM] * 3,
        grid=(1,),
    )(merging_weights, above, below, *ends, depth_weight, point_weight, mid)
    (stats,) = call(total_kernel, "statistics", [((16, 4, CH), f32)])(exchange(stats, PLANE))
    stats = exchange(stats, DEPTH)
    grad_fine, grad_coarse, send, grad_gain, grad_shift = call(
        backward_kernel,
        "backward",
        [
            (fine_level.shape, bf16),
            (coarse_level.shape, bf16),
            ((32, SLOT, LANES), bf16),
            ((1, CH), f32),
            ((1, CH), f32),
        ],
        [
            ((HEIGHT * WIDTH, CH), bf16),
            (((HEIGHT + 2) * WIDTH, CH), bf16),
            ((3, HEIGHT + 2, WIDTH, CH), f32),
            ((HEIGHT * HALF, CH), f32),
            ((3 * HEIGHT * HALF, LANES), f32),
            ((3 * CH, LANES), f32),
            ((32, SLOT, LANES), f32),
        ],
        [SMEM] + [VMEM] * 13,
    )(
        merging_weights, stats, above, below, fine_level, coarse_level, depth_weight, point_weight,
        norm_gain.reshape(1, CH), cotangent, depth_mid, depth_edge, proj_mid, proj_edge,
    )
    (part,) = call(relay_kernel, "sum_plane", [((16, SLOT, LANES), bf16)])(exchange(send, PLANE))
    (part,) = call(relay_kernel, "sum_depth", [((32, SLOT, LANES), bf16)])(exchange(part, DEPTH))
    grad_point, grad_depth, grad_merging = call(
        finish_kernel,
        "finish",
        [((CH, CH), bf16), ((3, 3, CH), f32), ((1, 2), f32)],
        [((3 * CH, LANES), f32)],
    )(exchange(part, PLANE))
    return (
        grad_fine,
        grad_coarse,
        grad_merging.reshape(2),
        grad_depth,
        grad_point,
        grad_gain.reshape(CH),
        grad_shift.reshape(CH),
    )


def solution(mesh):
    split = P("dp", "rows", None, None)
    return jax.shard_map(
        on_device,
        mesh=mesh,
        in_specs=(split, split, P(), P(), P(), P(), split),
        out_specs=(split, split, P(), P(), P(), P(), P()),
        check_vma=False,
    )
```

time: 151 us -> 127 us (0.84)
  blocking collectives: 15.5 us -> 47.2 us
  starting transfers between devices: 50.7 us -> 26.5 us
  local copies, waits for them, and re-layouts: 23.8 us -> 2.95 us
  other arithmetic: 20.7 us -> 1.19 us
  Pallas kernels: 0 us -> 9.58 us
  waiting for transfers between devices: 33.9 us -> 37.9 us
  matrix products: 2.14 us -> 0 us
  between operations: 2.84 us -> 0.78 us
    all_to_all x1 -> x3, blocking collectives: 15.5 us -> 47.2 us  [exchange(): return lax.all_to_all(parts, AXES, 0, 0, axis_index_groups=groups)]
    all_to_all x4 -> x2, starting transfers between devices: 39.2 us -> 15.4 us  [exchange(): return lax.all_to_all(parts, AXES, 0, 0, axis_index_groups=groups)]
    ppermute x1, waiting for transfers between devices: 0.01 us -> 17.4 us  [on_device(): below = lax.ppermute(head, 'rows', [(i + 1, i) for i in range(n - 1)])]
    all_to_all x4 -> x2, waiting for transfers between devices: 33.9 us -> 20.5 us  [exchange(): return lax.all_to_all(parts, AXES, 0, 0, axis_index_groups=groups)]
    pallas_call x0 -> x8, Pallas kernels: none -> 9.58 us  [the longest x1 4.13 us: on_device(): call(backward_kernel, 'backward', [(fine_level.shape, bf16), (coarse_leve...]
    slice x8 -> x0, local copies, waits for them, and re-layouts: 6.64 us -> none  [the longest x2 2.76 us: on_device(): up_ext[2:-2]]
    convert_element_type x12 -> x0, other arithmetic: 6.39 us -> none  [the longest x1 1.62 us: on_device(): grad_proj = (norm_gain * inv_std * (cot_ext - grad_shift / COUNT - normed...]
    broadcast_in_dim x3 -> x0, other arithmetic: 5.7 us -> none  [the longest x2 4.22 us: spread_to(): jnp.broadcast_to(block[None], (len(groups[0]),) + block.shape)]
  transfers between devices with their start and end apart: 6 -> 4, of which waited for: 4 -> 3; matrix products, arithmetic and copies ran while one was open for 9% -> 1% of each run, Pallas kernels for 0% -> 1%
where the time goes in v2:
time: 127 us; the launch traced here: 126 us
  blocking collectives  47.2 us (37%)
  waiting for transfers between devices  37.9 us (30%)
  starting transfers between devices  26.5 us (21%)
  Pallas kernels  9.58 us (8%)
  local copies, waits for them, and re-layouts  2.95 us (2%)
    all_to_all x3, blocking collectives, exchange(): return lax.all_to_all(parts, AXES, 0, 0, axis_index_groups=groups)  47.2 us
    all_to_all x2, waiting for transfers between devices, exchange(): return lax.all_to_all(parts, AXES, 0, 0, axis_index_groups=groups)  20.5 us
    ppermute x1, waiting for transfers between devices, on_device(): below = lax.ppermute(head, 'rows', [(i + 1, i) for i in range(n - 1)])  17.4 us
    all_to_all x2, starting transfers between devices, exchange(): return lax.all_to_all(parts, AXES, 0, 0, axis_index_groups=groups)  15.4 us
    ppermute x1, starting transfers between devices, on_device(): above = lax.ppermute(tail, 'rows', [(i, i + 1) for i in range(n - 1)])  9.78 us
    pallas_call x1, Pallas kernels, on_device(): call(backward_kernel, 'backward', [(fine_level.shape, bf16), (coarse_leve...  4.13 us
    unnamed x20, local copies, waits for them, and re-layouts  2.95 us
  transfers between devices with their start and end apart: 4, of which 3 were waited for; matrix products, arithmetic and copies ran while one was open for 1% of the time, Pallas kernels for 1%

profile of v2, /device:TPU:1, one launch (start us, length us, event | category | flops | bytes accessed | tf_op | source)
XLA Modules:
  0.0 126.1 jit_solution(1790891263939702347)
XLA Ops:
  0.6 0.0 copy-start
  0.6 1.0 copy-done
  1.7 1.0 copy-done.2
  2.7 0.9 copy-done.4
  3.6 0.0 copy-start.8
  3.6 9.8 %collective-permute-start = (bf16[168,384]{1,0:T(8,128)(2,1)S(1)}, bf16[168,384]{1,0:T(8,128)(2,1)S(1)}, u32[]{:S(2)}, u32[]{:S(2)}) collective-permute-start(bf16[168,384]{1,0:T(8,128)(2,1)S(1)} %get-tuple-element.23), channel_id=1, source_target_pairs={{0,1},{1,2},{2,3},{3,4},{4,5},{5,6},{6,7},{7,8},{8,9},{9,10},{10,1... | collective-permute-start | bytes 387080 | tf_op jit(solution)/shard_map/ppermute | solution.py:296
  13.4 1.3 %collective-permute-start.1 = (bf16[168,384]{1,0:T(8,128)(2,1)S(1)}, bf16[168,384]{1,0:T(8,128)(2,1)S(1)}, u32[]{:S(2)}, u32[]{:S(2)}) collective-permute-start(bf16[168,384]{1,0:T(8,128)(2,1)S(1)} %get-tuple-element.24), channel_id=1, source_target_pairs={{1,0},{2,1},{3,2},{4,3},{5,4},{6,5},{7,6},{8,7},{9,8},{10,9},{11,1... | collective-permute-start | bytes 387080 | tf_op jit(solution)/shard_map/ppermute | solution.py:297
  14.7 0.0 copy-done.6
  14.7 0.0 copy-done.7
  14.7 0.0 copy-done.8
  14.7 1.8 %middle.1 = (bf16[480,384]{1,0:T(8,128)(2,1)S(1)}, f32[480,384]{1,0:T(8,128)S(1)}, f32[4,384]{1,0:T(4,128)S(1)}) custom-call(f32[2]{0:T(128)S(1)} %copy-done.8, bf16[1,12,48,384]{3,2,1,0:T(8,128)(2,1)S(1)} %copy-done, bf16[1,6,24,384]{3,2,1,0:T(8,128)(2,1)S(1)} %copy-done.4, f32[3,3,384]{2,1,0:T(4,128)S(1)} %copy-done.7, bf16[384,384]{1,0:T(8,128)(2,1)S(1)} %copy-done.6, ...), custom_call_target="tpu_custom_call" | custom-call | flops 268435456 | bytes 1048576 | tf_op jit(solution)/shard_map/middle/pallas_call | solution.py:298
  16.5 0.0 collective-permute-done.above
  16.6 17.4 %collective-permute-done.1.below = bf16[168,384]{1,0:T(8,128)(2,1)S(1)} collective-permute-done((bf16[168,384]{1,0:T(8,128)(2,1)S(1)}, bf16[168,384]{1,0:T(8,128)(2,1)S(1)}, u32[]{:S(2)}, u32[]{:S(2)}) %collective-permute-start.1) | collective-permute-done | bytes 129056 | tf_op jit(solution)/shard_map/ppermute | solution.py:297
  33.9 1.3 %edge.1 = (bf16[192,384]{1,0:T(8,128)(2,1)S(1)}, f32[192,384]{1,0:T(8,128)S(1)}, f32[32,4,384]{2,1,0:T(4,128)S(1)}) custom-call(f32[2]{0:T(128)S(1)} %copy-done.8, bf16[168,384]{1,0:T(8,128)(2,1)S(1)} %collective-permute-done.above, bf16[168,384]{1,0:T(8,128)(2,1)S(1)} %collective-permute-done.1.below, bf16[1,12,48,384]{3,2,1,0:T(8,128)(2,1)S(1)} %copy-done, ...), custom_call_target="tpu_custom_call" | custom-call | bytes 1048576 | tf_op jit(solution)/shard_map/edge/pallas_call | solution.py:306
  35.3 0.0 copy-start.1
  35.3 0.0 copy-start.3
  35.3 16.3 %all_to_all.25.parts = f32[32,4,384]{2,1,0:T(4,128)S(1)} all-to-all(f32[32,4,384]{2,1,0:T(4,128)S(1)} %get-tuple-element.26), channel_id=1, replica_groups={{0,4,8,12,16,20,24,28,32,36,40,44,48,52,56,60,64,68,72,76,80,84,88,92,9..., dimensions={0} | all-to-all | bytes 393216 | tf_op jit(solution)/shard_map/all_to_all | solution.py:35
  51.6 0.7 statistics.1
  52.3 8.5 %all-to-all-start.1 = ((f32[16,4,384]{2,1,0:T(4,128)}), f32[16,4,384]{2,1,0:T(4,128)S(1)}, u32[]{:S(2)}, u32[]{:S(2)}) async-start(f32[16,4,384]{2,1,0:T(4,128)} %statistics.1), calls=%async_computation.1 | async-start | bytes 196608 | tf_op jit(solution)/shard_map/all_to_all | solution.py:35
  60.8 0.0 copy-done.9
  60.8 12.1 %all-to-all-done.1.gathered = f32[16,4,384]{2,1,0:T(4,128)S(1)} async-done(((f32[16,4,384]{2,1,0:T(4,128)}), f32[16,4,384]{2,1,0:T(4,128)S(1)}, u32[]{:S(2)}, u32[]{:S(2)}) %all-to-all-start.1) | async-done | bytes 98336 | tf_op jit(solution)/shard_map/all_to_all | solution.py:35
  72.9 0.0 copy-done.5
  72.9 4.1 %backward.1 = (bf16[1,12,48,384]{3,2,1,0:T(8,128)(2,1)}, bf16[1,6,24,384]{3,2,1,0:T(8,128)(2,1)}, bf16[32,40,128]{2,1,0:T(8,128)(2,1)S(1)}, f32[1,384]{1,0:T(1,128)S(1)}, f32[1,384]{1,0:T(1,128)S(1)}) custom-call(f32[2]{0:T(128)S(1)} %copy-done.8, f32[16,4,384]{2,1,0:T(4,128)S(1)} %all-to-all-done.1.gathered, ...), custom_call_target="tpu_custom_call" | custom-call | bytes 1048576 | tf_op jit(solution)/shard_map/backward/pallas_call | solution.py:316
  77.1 14.8 %all_to_all.26.parts = bf16[32,40,128]{2,1,0:T(8,128)(2,1)S(1)} all-to-all(bf16[32,40,128]{2,1,0:T(8,128)(2,1)S(1)} %get-tuple-element.33), channel_id=1, replica_groups={{0,4,8,12,16,20,24,28,32,36,40,44,48,52,56,60,64,68,72,76,80,84,88,92,9..., dimensions={0} | all-to-all | bytes 655360 | tf_op jit(solution)/shard_map/all_to_all | solution.py:35
  91.8 0.1 sum_plane.1
  91.9 16.1 %all_to_all.27.parts = bf16[16,40,128]{2,1,0:T(8,128)(2,1)S(1)} all-to-all(bf16[16,40,128]{2,1,0:T(8,128)(2,1)S(1)} %sum_plane.1), channel_id=1, replica_groups={{0,1,2,3,128,129,130,131,256,257,258,259,384,385,386,387},{4,5,6,7,132,..., dimensions={0} | all-to-all | bytes 327680 | tf_op jit(solution)/shard_map/all_to_all | solution.py:35
  108.0 0.8 sum_depth.1
  108.8 6.9 %all-to-all-start.4 = ((bf16[32,40,128]{2,1,0:T(8,128)(2,1)}), bf16[32,40,128]{2,1,0:T(8,128)(2,1)S(1)}, u32[]{:S(2)}, u32[]{:S(2)}) async-start(bf16[32,40,128]{2,1,0:T(8,128)(2,1)} %sum_depth.1), calls=%async_computation.4 | async-start | bytes 655360 | tf_op jit(solution)/shard_map/all_to_all | solution.py:35
  115.7 0.6 reduce
  116.3 0.6 reduce.1
  116.9 8.4 %all-to-all-done.4.parts = bf16[32,40,128]{2,1,0:T(8,128)(2,1)S(1)} async-done(((bf16[32,40,128]{2,1,0:T(8,128)(2,1)}), bf16[32,40,128]{2,1,0:T(8,128)(2,1)S(1)}, u32[]{:S(2)}, u32[]{:S(2)}) %all-to-all-start.4) | async-done | bytes 327712 | tf_op jit(solution)/shard_map/all_to_all | solution.py:35
  125.3 0.8 finish.1
  (10 shorter events, 0.0 us)
Async XLA Ops:
  0.6 1.0 copy-start
  1.6 1.0 copy-start.2
  2.7 0.9 copy-start.4
  3.6 11.1 %copy-start.6 = (bf16[384,384]{1,0:T(8,128)(2,1)S(1)}, bf16[384,384]{1,0:T(8,128)(2,1)}, u32[]{:S(2)}) copy-start(bf16[384,384]{1,0:T(8,128)(2,1)} %pw.5) | copy-start | bytes 884740
  3.6 11.1 %copy-start.7 = (f32[3,3,384]{2,1,0:T(4,128)S(1)}, f32[3,3,384]{2,1,0:T(4,128)}, u32[]{:S(2)}) copy-start(f32[3,3,384]{2,1,0:T(4,128)} %dw.5) | copy-start | bytes 41476
  3.6 11.1 %copy-start.8 = (f32[2]{0:T(128)S(1)}, f32[2]{0:T(128)}, u32[]{:S(2)}) copy-start(f32[2]{0:T(128)} %mw.5) | copy-start | bytes 28
  3.6 12.9 %collective-permute-start = (bf16[168,384]{1,0:T(8,128)(2,1)S(1)}, bf16[168,384]{1,0:T(8,128)(2,1)S(1)}, u32[]{:S(2)}, u32[]{:S(2)}) collective-permute-start(bf16[168,384]{1,0:T(8,128)(2,1)S(1)} %get-tuple-element.23), channel_id=1, source_target_pairs={{0,1},{1,2},{2,3},{3,4},{4,5},{5,6},{6,7},{7,8},{8,9},{9,10},{10,1... | collective-permute-start | bytes 387080 | tf_op jit(solution)/shard_map/ppermute | solution.py:296
  13.4 20.5 %collective-permute-start.1 = (bf16[168,384]{1,0:T(8,128)(2,1)S(1)}, bf16[168,384]{1,0:T(8,128)(2,1)S(1)}, u32[]{:S(2)}, u32[]{:S(2)}) collective-permute-start(bf16[168,384]{1,0:T(8,128)(2,1)S(1)} %get-tuple-element.24), channel_id=1, source_target_pairs={{1,0},{2,1},{3,2},{4,3},{5,4},{6,5},{7,6},{8,7},{9,8},{10,9},{11,1... | collective-permute-start | bytes 387080 | tf_op jit(solution)/shard_map/ppermute | solution.py:297
  33.9 26.9 %copy-start.9 = (f32[384]{0:T(512)S(1)}, f32[384]{0:T(512)}, u32[]{:S(2)}) copy-start(f32[384]{0:T(512)} %param.12) | copy-start | bytes 4612
  33.9 39.0 %copy-start.5 = (bf16[1,6,24,384]{3,2,1,0:T(8,128)(2,1)S(1)}, bf16[1,6,24,384]{3,2,1,0:T(8,128)(2,1)}, u32[]{:S(2)}) copy-start(bf16[1,6,24,384]{3,2,1,0:T(8,128)(2,1)} %coarse.3) | copy-start | bytes 331780
  35.3 37.7 %copy-start.1 = (bf16[1,12,48,384]{3,2,1,0:T(8,128)(2,1)S(1)}, bf16[1,12,48,384]{3,2,1,0:T(8,128)(2,1)}, u32[]{:S(2)}) copy-start(bf16[1,12,48,384]{3,2,1,0:T(8,128)(2,1)} %fine.3) | copy-start | bytes 1327108
  35.3 37.7 %copy-start.3 = (bf16[1,12,48,384]{3,2,1,0:T(8,128)(2,1)S(1)}, bf16[1,12,48,384]{3,2,1,0:T(8,128)(2,1)}, u32[]{:S(2)}) copy-start(bf16[1,12,48,384]{3,2,1,0:T(8,128)(2,1)} %cot.3) | copy-start | bytes 1327108
  52.3 20.6 %all-to-all-start.1 = ((f32[16,4,384]{2,1,0:T(4,128)}), f32[16,4,384]{2,1,0:T(4,128)S(1)}, u32[]{:S(2)}, u32[]{:S(2)}) async-start(f32[16,4,384]{2,1,0:T(4,128)} %statistics.1), calls=%async_computation.1 | async-start | bytes 196608 | tf_op jit(solution)/shard_map/all_to_all | solution.py:35
  108.8 16.5 %all-to-all-start.4 = ((bf16[32,40,128]{2,1,0:T(8,128)(2,1)}), bf16[32,40,128]{2,1,0:T(8,128)(2,1)S(1)}, u32[]{:S(2)}, u32[]{:S(2)}) async-start(bf16[32,40,128]{2,1,0:T(8,128)(2,1)} %sum_depth.1), calls=%async_computation.4 | async-start | bytes 655360 | tf_op jit(solution)/shard_map/all_to_all | solution.py:35

commit v3 on v2

v3 whole, which is shorter than its diff:
```python
import jax
import jax.numpy as jnp
from jax import lax
from jax.experimental import pallas as pl
from jax.experimental.pallas import tpu as pltpu
from jax.sharding import PartitionSpec as P

AXES = ("dp", "rows")
COUNT = 294912
HEIGHT, WIDTH, CH, LANES = 12, 48, 384, 128
HALF = WIDTH // 2
MID = HEIGHT - 2
PIECE = 36
SLOT = 40
bf16, f32 = jnp.bfloat16, jnp.float32


def groups_of(bits):
    rest = [b for b in range(9) if b not in bits]

    def spread(value, places):
        return sum(((value >> i) & 1) << b for i, b in enumerate(places))

    return [
        [spread(r, rest) + spread(m, bits) for m in range(1 << len(bits))]
        for r in range(1 << len(rest))
    ]


PLANE = groups_of([2, 3, 4, 5, 6])
DEPTH = groups_of([0, 1, 7, 8])


def exchange(parts, groups):
    return lax.all_to_all(parts, AXES, 0, 0, axis_index_groups=groups)


def column():
    return lax.broadcasted_iota(jnp.int32, (WIDTH, LANES), 0)


def from_left(x):
    return jnp.where(column() == 0, 0.0, pltpu.roll(x, 1, 0))


def from_right(x):
    return jnp.where(column() == WIDTH - 1, 0.0, pltpu.roll(x, WIDTH - 1, 0))


def shares(weights):
    first, second = jnp.full((1, LANES), weights[0]), jnp.full((1, LANES), weights[1])
    total = first + second + 0.0001
    return first / total, second / total, total


def doubled(coarse):
    n = coarse.shape[0]
    row = lax.broadcasted_iota(jnp.int32, (2 * n, n), 0)
    place = lax.broadcasted_iota(jnp.int32, (2 * n, n), 1)
    pick = jnp.where((row == 2 * place) | (row == 2 * place + 1), 1.0, 0.0).astype(bf16)
    return jnp.dot(pick, coarse, preferred_element_type=f32)


def blocks():
    return [slice(c * LANES, (c + 1) * LANES) for c in range(CH // LANES)]


def activate(fine, up, share):
    merged = share[0] * fine + share[1] * up
    sig = jax.nn.sigmoid(merged)
    return merged, sig, (merged * sig).astype(bf16).astype(f32)


def convolve(rows, taps, dw, c):
    across = [sum(row * dw[a, b : b + 1, c] for row, a in zip(rows, taps)) for b in range(3)]
    return from_left(across[0]) + across[1] + from_right(across[2])


def folded(x):
    return jnp.sum(x.reshape(-1, 8, x.shape[-1]), axis=0)


def statistics(proj, cot):
    parts = (proj, proj * proj, cot, cot * proj)
    return [jnp.sum(folded(p), axis=0, keepdims=True) for p in parts]


def pack_kernel(mw, ft, fb, ct, cb, gt, gb, head, tail):
    share = shares(mw)
    for out, fine, coarse, cot, rows in ((head, ft, ct, gt, (0, 1)), (tail, fb, cb, gb, (1, 0))):
        up = doubled(coarse[0, 0])
        for k, r in enumerate(rows):
            for c in blocks():
                act = activate(fine[0, r, :, c].astype(f32), up[:, c], share)[2]
                out[k * WIDTH : (k + 1) * WIDTH, c] = act.astype(bf16)
        out[2 * WIDTH : 3 * WIDTH] = cot[0, 0]


def factors(row, up, share):
    merged, sig, act = activate(row, up, share)
    slope = sig * (1.0 + merged * (1.0 - sig))
    return act, slope, ((row - merged) / share[2], (up - merged) / share[2])


def middle_kernel(
    mw, fine, coarse, dw, pw, cot, depth, proj, stats, partial, act, factor, slope, up
):
    share = shares(mw)
    up[...] = doubled(coarse[0].reshape(-1, CH))
    last = HEIGHT - 1
    for c in blocks():
        for i in range(HEIGHT):
            u = up[(i // 2) * WIDTH : (i // 2 + 1) * WIDTH, c]
            found = factors(fine[0, i, :, c].astype(f32), u, share)
            act[i, :, c], slope[i, :, c], (factor[0, i, :, c], factor[1, i, :, c]) = found
        for i in range(HEIGHT):
            taps = [a for a in range(3) if 0 <= i + a - 1 <= last]
            sums = convolve([act[i + a - 1, :, c] for a in taps], taps, dw, c)
            if 0 < i < last:
                depth[(i - 1) * WIDTH : i * WIDTH, c] = sums.astype(bf16)
            else:
                partial[i // last, :, c] = sums
    proj[...] = jnp.dot(depth[...], pw[...], preferred_element_type=f32)
    own = cot[0, 1:last].reshape(-1, CH).astype(f32)
    for k, s in enumerate(statistics(proj[...], own)):
        stats[k : k + 1] = s


def edge_kernel(above, below, partial, act, gt, gb, dw, pw, mid, depth, proj, stats):
    for e, (halo, a) in enumerate(((above, 0), (below, 2))):
        for c in blocks():
            near = halo[0:WIDTH, c].astype(f32)
            far = halo[WIDTH : 2 * WIDTH, c].astype(f32)
            inner = partial[e, :, c] + convolve((near,), (a,), dw, c)
            rows = (far, near, act[0, :, c]) if e == 0 else (act[HEIGHT - 1, :, c], near, far)
            outer = convolve(rows, range(3), dw, c)
            for k, row in enumerate((outer, inner) if e == 0 else (inner, outer)):
                at = (2 * e + k) * WIDTH
                depth[at : at + WIDTH, c] = row.astype(bf16)
    proj[...] = jnp.dot(depth[...], pw[...], preferred_element_type=f32)
    first = statistics(proj[WIDTH : 2 * WIDTH], gt[0, 0].astype(f32))
    last = statistics(proj[2 * WIDTH : 3 * WIDTH], gb[0, 0].astype(f32))
    whole = jnp.concatenate([x + y for x, y in zip(first, last)], axis=0) + mid[...]
    stats[...] = jnp.broadcast_to(whole[None], stats.shape)


def total_kernel(parts, out):
    out[...] = jnp.broadcast_to(jnp.sum(parts[...], axis=0)[None], out.shape)


def gradient_kernel(
    gathered, above, below, cot, pw, gain, depth_mid, depth_edge, proj_mid, proj_edge, act,
    send, grad_gain, grad_shift, gmap, own_depth, gproj, point, slots,
):
    n, end = 2 * WIDTH, HEIGHT * WIDTH
    stats = jnp.sum(gathered[...], axis=0)
    mean = stats[0:1] / COUNT
    variance = stats[1:2] / COUNT - mean * mean
    inv_std = 1.0 / jnp.sqrt(variance + 1e-05)
    shift = stats[2:3]
    gained = inv_std * (stats[3:4] - mean * shift)
    grad_gain[...] = gained
    grad_shift[...] = shift
    scale = gain[...] * inv_std
    by_proj = -(scale * inv_std * gained) / COUNT
    offset = -(scale * shift) / COUNT

    def gradient(g, p):
        return (scale * g.astype(f32) + (by_proj * (p - mean) + offset)).astype(bf16)

    gproj[0:WIDTH] = gradient(above[n : n + WIDTH], proj_edge[0:WIDTH])
    gproj[WIDTH:n] = gradient(cot[0, 0], proj_edge[WIDTH:n])
    mid_cot = cot[0, 1 : HEIGHT - 1].reshape(-1, CH)
    gproj[n:end] = gradient(mid_cot, proj_mid[...])
    gproj[end : end + WIDTH] = gradient(cot[0, HEIGHT - 1], proj_edge[n : n + WIDTH])
    gproj[end + WIDTH : end + n] = gradient(below[n : n + WIDTH], proj_edge[n + WIDTH : 2 * n])
    own_depth[0:WIDTH] = depth_edge[WIDTH:n]
    own_depth[WIDTH : end - WIDTH] = depth_mid[...]
    own_depth[end - WIDTH : end] = depth_edge[n : n + WIDTH]
    gmap[...] = lax.dot_general(
        gproj[...], pw[...], (((1,), (1,)), ((), ())), preferred_element_type=f32
    ).astype(bf16)
    whole_point = lax.dot_general(
        own_depth[...], gproj[WIDTH : end + WIDTH], (((0,), (0,)), ((), ())),
        preferred_element_type=f32,
    )
    zero = jnp.zeros((1, LANES), f32)
    small = [zero] * 32
    for k, c in enumerate(blocks()):
        point[k * CH : (k + 1) * CH] = whole_point[:, c]
        taps = [jnp.zeros((8, LANES), f32)] * 9
        ends = [halo[0:WIDTH, c].astype(f32) for halo in (above, below)]
        for i in range(HEIGHT):
            x = gmap[(i + 1) * WIDTH : (i + 2) * WIDTH, c].astype(f32)
            moved = from_right(x), x, from_left(x)
            for a in range(3):
                r = i + a - 1
                row = ends[0] if r < 0 else ends[1] if r == HEIGHT else act[r, :, c]
                for b in range(3):
                    taps[3 * a + b] = taps[3 * a + b] + folded(row * moved[b])
        for t in range(9):
            small[3 * t + k] = jnp.sum(taps[t], axis=0, keepdims=True)
    for s in range(32):
        slots[s, 0:PIECE] = point[s * PIECE : (s + 1) * PIECE]
        high = small[s].astype(bf16).astype(f32)
        slots[s, PIECE:SLOT] = jnp.concatenate([high, small[s] - high, zero, zero], axis=0)
    send[...] = slots[...].astype(bf16)


def level_kernel(
    mw, gmap, slope, factor, dw, grad_fine, grad_coarse, merging, moved, pairs
):
    share = shares(mw)
    m = HEIGHT * HALF // 2
    place = lax.axis_index("rows")
    keep = {
        0: jnp.where(place == 0, 0.0, 1.0),
        HEIGHT + 1: jnp.where(place == lax.axis_size("rows") - 1, 0.0, 1.0),
    }
    by_weight = [jnp.zeros((8, LANES), f32)] * 2
    for k, c in enumerate(blocks()):
        for r in range(HEIGHT + 2):
            x = gmap[r * WIDTH : (r + 1) * WIDTH, c].astype(f32)
            x = x * keep[r] if r in keep else x
            moved[0, r, :, c] = from_right(x)
            moved[1, r, :, c] = x
            moved[2, r, :, c] = from_left(x)
        for p in range(HEIGHT):
            grad_act = jnp.zeros((WIDTH, LANES), f32)
            for a in range(3):
                for b in range(3):
                    grad_act = grad_act + moved[b, p + 2 - a, :, c] * dw[a, b : b + 1, c]
            grad_merged = grad_act * slope[p, :, c]
            for t in range(2):
                by_weight[t] = by_weight[t] + folded(grad_merged * factor[t, p, :, c])
            grad_fine[0, p, :, c] = (grad_merged * share[0]).astype(bf16)
            at = 2 * k * m + (p // 2) * WIDTH
            if p % 2 == 0:
                pairs[at : at + WIDTH] = grad_merged
            else:
                pairs[at : at + WIDTH] = pairs[at : at + WIDTH] + grad_merged
        both = pairs[pl.ds(2 * k * m, m, stride=2)] + pairs[pl.ds(2 * k * m + 1, m, stride=2)]
        grad_coarse[0, :, :, c] = (both * share[1]).astype(bf16).reshape(HEIGHT // 2, HALF, LANES)
    lane = lax.broadcasted_iota(jnp.int32, (1, LANES), 1)
    first, second = [
        jnp.sum(jnp.sum(x, axis=0, keepdims=True), axis=1, keepdims=True) for x in by_weight
    ]
    merging[...] = jnp.where(lane == 0, first, jnp.where(lane == 1, second, 0.0))


def relay_kernel(parts, *refs):
    out = refs[-1]
    total = jnp.sum(parts[...].astype(f32), axis=0)
    row = lax.broadcasted_iota(jnp.int32, (SLOT, LANES), 0)
    for at in (PIECE, PIECE + 2):
        value = total[at : at + 1] + total[at + 1 : at + 2]
        if at > PIECE and len(refs) > 1:
            value = refs[0][...]
        high = value.astype(bf16).astype(f32)
        total = jnp.where(row == at, high, jnp.where(row == at + 1, value - high, total))
    out[...] = jnp.broadcast_to(total.astype(bf16)[None], out.shape)


def finish_kernel(parts, grad_point, grad_depth, grad_merging, point):
    rest, merging = [], jnp.zeros((1, LANES), f32)
    for s in range(32):
        slot = parts[s].astype(f32)
        point[s * PIECE : (s + 1) * PIECE] = slot[0:PIECE]
        rest.append(slot[PIECE : PIECE + 1] + slot[PIECE + 1 : PIECE + 2])
        merging = merging + (slot[PIECE + 2 : PIECE + 3] + slot[PIECE + 3 : PIECE + 4])
    for k, c in enumerate(blocks()):
        grad_point[:, c] = point[k * CH : (k + 1) * CH].astype(bf16)
        for t in range(9):
            grad_depth[t // 3, t % 3 : t % 3 + 1, c] = rest[3 * t + k]
    grad_merging[...] = merging[:, 0:2]


VMEM = pl.BlockSpec(memory_space=pltpu.VMEM)
SMEM = pl.BlockSpec(memory_space=pltpu.SMEM)


def call(kernel, name, outs, scratch=(), in_specs=None, cost=0, grid=(), limit=32):
    return pl.pallas_call(
        kernel,
        name=name,
        grid=grid,
        out_shape=[jax.ShapeDtypeStruct(s, t) for s, t in outs],
        in_specs=in_specs or [VMEM],
        out_specs=[VMEM] * len(outs),
        scratch_shapes=[pltpu.VMEM(s, t) for s, t in scratch],
        compiler_params=pltpu.CompilerParams(vmem_limit_bytes=limit << 20),
        cost_estimate=pl.CostEstimate(flops=cost, bytes_accessed=1 << 20, transcendentals=0),
    )


def at(shape, row):
    return pl.BlockSpec(shape, lambda i: (0, row, 0, 0))


FINE, COARSE, COT = (1, 2, WIDTH, CH), (1, 1, HALF, CH), (1, 1, WIDTH, CH)
COT_ENDS = [at(COT, 0), at(COT, HEIGHT - 1)]
FINE_ENDS = [at(FINE, 0), at(FINE, HEIGHT // 2 - 1)]
COARSE_ENDS = [at(COARSE, 0), at(COARSE, HEIGHT // 2 - 1)]


def on_device(
    fine_level, coarse_level, merging_weights, depth_weight, point_weight, norm_gain, cotangent
):
    ends = (fine_level, fine_level, coarse_level, coarse_level, cotangent, cotangent)
    head, tail = call(
        pack_kernel,
        "pack",
        [((3 * WIDTH, CH), bf16)] * 2,
        in_specs=[SMEM] + FINE_ENDS + COARSE_ENDS + COT_ENDS,
        grid=(1,),
        limit=56,
    )(merging_weights, *ends)
    n = lax.axis_size("rows")
    above = lax.ppermute(tail, "rows", [(i, i + 1) for i in range(n - 1)])
    below = lax.ppermute(head, "rows", [(i + 1, i) for i in range(n - 1)])
    whole = ((HEIGHT, WIDTH, CH), f32)
    depth_mid, proj_mid, mid, partial, act, factor, slope = call(
        middle_kernel,
        "middle",
        [
            ((MID * WIDTH, CH), bf16),
            ((MID * WIDTH, CH), f32),
            ((4, CH), f32),
            ((2, WIDTH, CH), f32),
            whole,
            ((2,) + whole[0], f32),
            whole,
        ],
        [((HEIGHT * HALF, CH), f32)],
        [SMEM] + [VMEM] * 5,
        cost=1 << 28,
    )(merging_weights, fine_level, coarse_level, depth_weight, point_weight, cotangent)
    depth_edge, proj_edge, stats = call(
        edge_kernel,
        "edge",
        [((4 * WIDTH, CH), bf16), ((4 * WIDTH, CH), f32), ((32, 4, CH), f32)],
        [],
        [VMEM] * 4 + COT_ENDS + [VMEM] * 3,
        grid=(1,),
    )(above, below, partial, act, cotangent, cotangent, depth_weight, point_weight, mid)
    (stats,) = call(total_kernel, "statistics", [((16, 4, CH), f32)])(exchange(stats, PLANE))
    send, grad_gain, grad_shift, gmap = call(
        gradient_kernel,
        "gradient",
        [
            ((32, SLOT, LANES), bf16),
            ((1, CH), f32),
            ((1, CH), f32),
            (((HEIGHT + 2) * WIDTH, CH), bf16),
        ],
        [
            ((HEIGHT * WIDTH, CH), bf16),
            (((HEIGHT + 2) * WIDTH, CH), bf16),
            ((3 * CH, LANES), f32),
            ((32, SLOT, LANES), f32),
        ],
        [VMEM] * 11,
    )(
        exchange(stats, DEPTH), above, below, cotangent, point_weight, norm_gain.reshape(1, CH),
        depth_mid, depth_edge, proj_mid, proj_edge, act,
    )
    grad_fine, grad_coarse, merging = call(
        level_kernel,
        "levels",
        [(fine_level.shape, bf16), (coarse_level.shape, bf16), ((1, LANES), f32)],
        [((3, HEIGHT + 2, WIDTH, CH), f32), ((3 * HEIGHT * HALF, LANES), f32)],
        [SMEM] + [VMEM] * 4,
        cost=1 << 28,
        limit=56,
    )(merging_weights, gmap, slope, factor, depth_weight)
    (part,) = call(
        relay_kernel, "sum_plane", [((16, SLOT, LANES), bf16)], in_specs=[VMEM] * 2
    )(exchange(send, PLANE), merging)
    (part,) = call(relay_kernel, "sum_depth", [((32, SLOT, LANES), bf16)])(exchange(part, DEPTH))
    grad_point, grad_depth, grad_merging = call(
        finish_kernel,
        "finish",
        [((CH, CH), bf16), ((3, 3, CH), f32), ((1, 2), f32)],
        [((3 * CH, LANES), f32)],
    )(exchange(part, PLANE))
    return (
        grad_fine,
        grad_coarse,
        grad_merging.reshape(2),
        grad_depth,
        grad_point,
        grad_gain.reshape(CH),
        grad_shift.reshape(CH),
    )


def solution(mesh):
    split = P("dp", "rows", None, None)
    return jax.shard_map(
        on_device,
        mesh=mesh,
        in_specs=(split, split, P(), P(), P(), P(), split),
        out_specs=(split, split, P(), P(), P(), P(), P()),
        check_vma=False,
    )
```

time: 127 us -> 123 us (0.969)
  blocking collectives: 47.2 us -> 32.2 us
  starting transfers between devices: 26.5 us -> 32.2 us
  Pallas kernels: 9.58 us -> 12.7 us
  waiting for transfers between devices: 37.9 us -> 40 us
    all_to_all x3 -> x2, blocking collectives: 47.2 us -> 32.2 us  [exchange(): return lax.all_to_all(parts, AXES, 0, 0, axis_index_groups=groups)]
    all_to_all x2 -> x3, waiting for transfers between devices: 20.5 us -> 26.4 us  [exchange(): return lax.all_to_all(parts, AXES, 0, 0, axis_index_groups=groups)]
    all_to_all x2 -> x3, starting transfers between devices: 15.4 us -> 21.2 us  [exchange(): return lax.all_to_all(parts, AXES, 0, 0, axis_index_groups=groups)]
    ppermute x1, waiting for transfers between devices: 17.4 us -> 13.6 us  [on_device(): below = lax.ppermute(head, 'rows', [(i + 1, i) for i in range(n - 1)])]
    pallas_call x3 -> x4, Pallas kernels: 4.22 us -> 7.98 us  [the longest x1 3.69 us: on_device(): call(level_kernel, 'levels', [(fine_level.shape, bf16), (coarse_level.sha...]
    unnamed x20 -> x22, local copies, waits for them, and re-layouts: 2.95 us -> 3.62 us
  transfers between devices with their start and end apart: 4 -> 5, of which waited for: 3 -> 4; matrix products, arithmetic and copies ran while one was open for 1% -> 1% of each run, Pallas kernels for 1% -> 5%
where the time goes in v3:
time: 123 us
  waiting for transfers between devices  40 us (33%)
  starting transfers between devices  32.2 us (26%)
  blocking collectives  32.2 us (26%)
  Pallas kernels  12.7 us (10%)
  local copies, waits for them, and re-layouts  3.62 us (3%)
    all_to_all x2, blocking collectives, exchange(): return lax.all_to_all(parts, AXES, 0, 0, axis_index_groups=groups)  32.2 us
    all_to_all x3, waiting for transfers between devices, exchange(): return lax.all_to_all(parts, AXES, 0, 0, axis_index_groups=groups)  26.4 us
    all_to_all x3, starting transfers between devices, exchange(): return lax.all_to_all(parts, AXES, 0, 0, axis_index_groups=groups)  21.2 us
    ppermute x1, waiting for transfers between devices, on_device(): below = lax.ppermute(head, 'rows', [(i + 1, i) for i in range(n - 1)])  13.6 us
    ppermute x1, starting transfers between devices, on_device(): above = lax.ppermute(tail, 'rows', [(i, i + 1) for i in range(n - 1)])  9.64 us
    pallas_call x1, Pallas kernels, on_device(): call(level_kernel, 'levels', [(fine_level.shape, bf16), (coarse_level.sha...  3.69 us
    unnamed x22, local copies, waits for them, and re-layouts  3.62 us
  transfers between devices with their start and end apart: 5, of which 4 were waited for; matrix products, arithmetic and copies ran while one was open for 1% of the time, Pallas kernels for 5%

profile of v3, /device:TPU:1, one launch (start us, length us, event | category | flops | bytes accessed | tf_op | source)
XLA Modules:
  0.0 122.8 jit_solution(13179271889353977389)
XLA Ops:
  0.6 0.0 copy-start
  0.6 0.0 copy-start.8
  0.7 0.0 copy-start.4
  0.7 0.0 copy-start.1
  0.7 0.0 copy-start.7
  0.7 1.9 %pack.1 = (bf16[144,384]{1,0:T(8,128)(2,1)}, bf16[144,384]{1,0:T(8,128)(2,1)}) custom-call(f32[2]{0:T(128)} %mw.5, bf16[1,12,48,384]{3,2,1,0:T(8,128)(2,1)} %fine.1, bf16[1,12,48,384]{3,2,1,0:T(8,128)(2,1)} %fine.1, bf16[1,6,24,384]{3,2,1,0:T(8,128)(2,1)} %coarse.1, bf16[1,6,24,384]{3,2,1,0:T(8,128)(2,1)} %coarse.1, bf16[1,12,48,384]{3,2,1,0:T(8,128)(2,1)} %cot.3, ...), custom_call_target="tpu_custom_call" | custom-call | bytes 1048576 | tf_op jit(solution)/shard_map/pack/pallas_call | solution.py:310
  2.6 9.6 %collective-permute-start = (bf16[144,384]{1,0:T(8,128)(2,1)}, bf16[144,384]{1,0:T(8,128)(2,1)S(1)}, u32[]{:S(2)}, u32[]{:S(2)}) collective-permute-start(bf16[144,384]{1,0:T(8,128)(2,1)} %get-tuple-element.29), channel_id=1, source_target_pairs={{0,1},{1,2},{2,3},{3,4},{4,5},{5,6},{6,7},{7,8},{8,9},{9,10},{10,1... | collective-permute-start | bytes 331784 | tf_op jit(solution)/shard_map/ppermute | solution.py:319
  12.2 1.3 %collective-permute-start.1 = (bf16[144,384]{1,0:T(8,128)(2,1)}, bf16[144,384]{1,0:T(8,128)(2,1)S(1)}, u32[]{:S(2)}, u32[]{:S(2)}) collective-permute-start(bf16[144,384]{1,0:T(8,128)(2,1)} %get-tuple-element.30), channel_id=1, source_target_pairs={{1,0},{2,1},{3,2},{4,3},{5,4},{6,5},{7,6},{8,7},{9,8},{10,9},{11,1... | collective-permute-start | bytes 331784 | tf_op jit(solution)/shard_map/ppermute | solution.py:320
  13.6 2.1 %middle.1 = (bf16[480,384]{1,0:T(8,128)(2,1)S(1)}, f32[480,384]{1,0:T(8,128)S(1)}, f32[4,384]{1,0:T(4,128)S(1)}, f32[2,48,384]{2,1,0:T(8,128)S(1)}, f32[12,48,38...) custom-call(f32[2]{0:T(128)S(1)} %copy-done.8, bf16[1,12,48,384]{3,2,1,0:T(8,128)(2,1)S(1)} %copy-done.1, ...), custom_call_target="tpu_custom_call" | custom-call | flops 268435456 | bytes 1048576 | tf_op jit(solution)/shard_map/middle/pallas_call | solution.py:322
  15.7 1.2 copy-done.3
  16.9 0.9 copy-done.5
  17.8 0.0 collective-permute-done.above
  17.8 13.6 %collective-permute-done.1.below = bf16[144,384]{1,0:T(8,128)(2,1)S(1)} collective-permute-done((bf16[144,384]{1,0:T(8,128)(2,1)}, bf16[144,384]{1,0:T(8,128)(2,1)S(1)}, u32[]{:S(2)}, u32[]{:S(2)}) %collective-permute-start.1) | collective-permute-done | bytes 110624 | tf_op jit(solution)/shard_map/ppermute | solution.py:320
  31.4 0.4 edge.1
  31.8 16.2 %all_to_all.25.parts = f32[32,4,384]{2,1,0:T(4,128)S(1)} all-to-all(f32[32,4,384]{2,1,0:T(4,128)S(1)} %get-tuple-element.34), channel_id=1, replica_groups={{0,4,8,12,16,20,24,28,32,36,40,44,48,52,56,60,64,68,72,76,80,84,88,92,9..., dimensions={0} | all-to-all | bytes 393216 | tf_op jit(solution)/shard_map/all_to_all | solution.py:35
  48.0 0.7 statistics.1
  48.7 8.4 %all-to-all-start.1 = ((f32[16,4,384]{2,1,0:T(4,128)}), f32[16,4,384]{2,1,0:T(4,128)S(1)}, u32[]{:S(2)}, u32[]{:S(2)}) async-start(f32[16,4,384]{2,1,0:T(4,128)} %statistics.1), calls=%async_computation.1 | async-start | bytes 196608 | tf_op jit(solution)/shard_map/all_to_all | solution.py:35
  57.1 12.1 %all-to-all-done.1.gathered = f32[16,4,384]{2,1,0:T(4,128)S(1)} async-done(((f32[16,4,384]{2,1,0:T(4,128)}), f32[16,4,384]{2,1,0:T(4,128)S(1)}, u32[]{:S(2)}, u32[]{:S(2)}) %all-to-all-start.1) | async-done | bytes 98336 | tf_op jit(solution)/shard_map/all_to_all | solution.py:35
  69.2 2.3 %gradient.1 = (bf16[32,40,128]{2,1,0:T(8,128)(2,1)}, f32[1,384]{1,0:T(1,128)S(1)}, f32[1,384]{1,0:T(1,128)S(1)}, bf16[672,384]{1,0:T(8,128)(2,1)S(1)}) custom-call(f32[16,4,384]{2,1,0:T(4,128)S(1)} %all-to-all-done.1.gathered, bf16[144,384]{1,0:T(8,128)(2,1)S(1)} %collective-permute-done.above, bf16[144,384]{1,0:T(8,128)(2,1)S(1)} %collective-permute-done.1.below, ...), custom_call_target="tpu_custom_call" | custom-call | bytes 1048576 | tf_op jit(solution)/shard_map/gradient/pallas_call | solution.py:347
  71.5 0.8 copy-done.6
  72.3 6.0 %all-to-all-start.2 = ((bf16[32,40,128]{2,1,0:T(8,128)(2,1)}), bf16[32,40,128]{2,1,0:T(8,128)(2,1)S(1)}, u32[]{:S(2)}, u32[]{:S(2)}) async-start(bf16[32,40,128]{2,1,0:T(8,128)(2,1)} %get-tuple-element.44), calls=%async_computation.2 | async-start | bytes 655360 | tf_op jit(solution)/shard_map/all_to_all | solution.py:35
  78.3 3.7 %levels.1 = (bf16[1,12,48,384]{3,2,1,0:T(8,128)(2,1)}, bf16[1,6,24,384]{3,2,1,0:T(8,128)(2,1)}, f32[1,128]{1,0:T(1,128)}) custom-call(f32[2]{0:T(128)} %mw.5, bf16[672,384]{1,0:T(8,128)(2,1)} %copy-done.6, f32[12,48,384]{2,1,0:T(8,128)} %copy-done.5, f32[2,12,48,384]{3,2,1,0:T(8,128)} %copy-done.3, f32[3,3,384]{2,1,0:T(4,128)} %dw.5), custom_call_target="tpu_custom_call" | custom-call | flops 268435456 | bytes 1048576 | tf_op jit(solution)/shard_map/levels/pallas_call | solution.py:367
  82.0 5.9 %all-to-all-done.2.parts = bf16[32,40,128]{2,1,0:T(8,128)(2,1)S(1)} async-done(((bf16[32,40,128]{2,1,0:T(8,128)(2,1)}), bf16[32,40,128]{2,1,0:T(8,128)(2,1)S(1)}, u32[]{:S(2)}, u32[]{:S(2)}) %all-to-all-start.2) | async-done | bytes 327712 | tf_op jit(solution)/shard_map/all_to_all | solution.py:35
  87.9 0.7 copy-done.9
  88.6 0.1 sum_plane.1
  88.7 16.1 %all_to_all.26.parts = bf16[16,40,128]{2,1,0:T(8,128)(2,1)S(1)} all-to-all(bf16[16,40,128]{2,1,0:T(8,128)(2,1)S(1)} %sum_plane.1), channel_id=1, replica_groups={{0,1,2,3,128,129,130,131,256,257,258,259,384,385,386,387},{4,5,6,7,132,..., dimensions={0} | all-to-all | bytes 327680 | tf_op jit(solution)/shard_map/all_to_all | solution.py:35
  104.7 0.8 sum_depth.1
  105.5 6.9 %all-to-all-start.4 = ((bf16[32,40,128]{2,1,0:T(8,128)(2,1)}), bf16[32,40,128]{2,1,0:T(8,128)(2,1)S(1)}, u32[]{:S(2)}, u32[]{:S(2)}) async-start(bf16[32,40,128]{2,1,0:T(8,128)(2,1)} %sum_depth.1), calls=%async_computation.4 | async-start | bytes 655360 | tf_op jit(solution)/shard_map/all_to_all | solution.py:35
  112.4 0.6 reduce
  113.0 0.6 reduce.1
  113.6 8.4 %all-to-all-done.4.parts = bf16[32,40,128]{2,1,0:T(8,128)(2,1)S(1)} async-done(((bf16[32,40,128]{2,1,0:T(8,128)(2,1)}), bf16[32,40,128]{2,1,0:T(8,128)(2,1)S(1)}, u32[]{:S(2)}, u32[]{:S(2)}) %all-to-all-start.4) | async-done | bytes 327712 | tf_op jit(solution)/shard_map/all_to_all | solution.py:35
  122.0 0.8 finish.1
  (14 shorter events, 0.0 us)
Async XLA Ops:
  0.6 12.9 %copy-start = (bf16[1,12,48,384]{3,2,1,0:T(8,128)(2,1)S(1)}, bf16[1,12,48,384]{3,2,1,0:T(8,128)(2,1)}, u32[]{:S(2)}) copy-start(bf16[1,12,48,384]{3,2,1,0:T(8,128)(2,1)} %cot.3) | copy-start | bytes 1327108
  0.6 12.9 %copy-start.8 = (f32[2]{0:T(128)S(1)}, f32[2]{0:T(128)}, u32[]{:S(2)}) copy-start(f32[2]{0:T(128)} %mw.5) | copy-start | bytes 28
  0.7 12.9 %copy-start.4 = (bf16[1,6,24,384]{3,2,1,0:T(8,128)(2,1)S(1)}, bf16[1,6,24,384]{3,2,1,0:T(8,128)(2,1)}, u32[]{:S(2)}) copy-start(bf16[1,6,24,384]{3,2,1,0:T(8,128)(2,1)} %coarse.1) | copy-start | bytes 331780
  0.7 12.9 %copy-start.1 = (bf16[1,12,48,384]{3,2,1,0:T(8,128)(2,1)S(1)}, bf16[1,12,48,384]{3,2,1,0:T(8,128)(2,1)}, u32[]{:S(2)}) copy-start(bf16[1,12,48,384]{3,2,1,0:T(8,128)(2,1)} %fine.1) | copy-start | bytes 1327108
  0.7 12.9 %copy-start.2 = (bf16[384,384]{1,0:T(8,128)(2,1)S(1)}, bf16[384,384]{1,0:T(8,128)(2,1)}, u32[]{:S(2)}) copy-start(bf16[384,384]{1,0:T(8,128)(2,1)} %pw.5) | copy-start | bytes 884740
  0.7 12.9 %copy-start.7 = (f32[3,3,384]{2,1,0:T(4,128)S(1)}, f32[3,3,384]{2,1,0:T(4,128)}, u32[]{:S(2)}) copy-start(f32[3,3,384]{2,1,0:T(4,128)} %dw.5) | copy-start | bytes 41476
  2.6 15.2 %collective-permute-start = (bf16[144,384]{1,0:T(8,128)(2,1)}, bf16[144,384]{1,0:T(8,128)(2,1)S(1)}, u32[]{:S(2)}, u32[]{:S(2)}) collective-permute-start(bf16[144,384]{1,0:T(8,128)(2,1)} %get-tuple-element.29), channel_id=1, source_target_pairs={{0,1},{1,2},{2,3},{3,4},{4,5},{5,6},{6,7},{7,8},{8,9},{9,10},{10,1... | collective-permute-start | bytes 331784 | tf_op jit(solution)/shard_map/ppermute | solution.py:319
  12.2 19.2 %collective-permute-start.1 = (bf16[144,384]{1,0:T(8,128)(2,1)}, bf16[144,384]{1,0:T(8,128)(2,1)S(1)}, u32[]{:S(2)}, u32[]{:S(2)}) collective-permute-start(bf16[144,384]{1,0:T(8,128)(2,1)} %get-tuple-element.30), channel_id=1, source_target_pairs={{1,0},{2,1},{3,2},{4,3},{5,4},{6,5},{7,6},{8,7},{9,8},{10,9},{11,1... | collective-permute-start | bytes 331784 | tf_op jit(solution)/shard_map/ppermute | solution.py:320
  15.7 1.2 %copy-start.3 = (f32[2,12,48,384]{3,2,1,0:T(8,128)}, f32[2,12,48,384]{3,2,1,0:T(8,128)S(1)}, u32[]{:S(2)}) copy-start(f32[2,12,48,384]{3,2,1,0:T(8,128)S(1)} %get-tuple-element.41.factor) | copy-start | bytes 5308420
  16.9 0.9 copy-start.5
  17.8 39.3 %copy-start.10 = (f32[384]{0:T(512)S(1)}, f32[384]{0:T(512)}, u32[]{:S(2)}) copy-start(f32[384]{0:T(512)} %param.12) | copy-start | bytes 4612
  48.7 20.5 %all-to-all-start.1 = ((f32[16,4,384]{2,1,0:T(4,128)}), f32[16,4,384]{2,1,0:T(4,128)S(1)}, u32[]{:S(2)}, u32[]{:S(2)}) async-start(f32[16,4,384]{2,1,0:T(4,128)} %statistics.1), calls=%async_computation.1 | async-start | bytes 196608 | tf_op jit(solution)/shard_map/all_to_all | solution.py:35
  71.5 0.8 copy-start.6
  72.3 15.6 %all-to-all-start.2 = ((bf16[32,40,128]{2,1,0:T(8,128)(2,1)}), bf16[32,40,128]{2,1,0:T(8,128)(2,1)S(1)}, u32[]{:S(2)}, u32[]{:S(2)}) async-start(bf16[32,40,128]{2,1,0:T(8,128)(2,1)} %get-tuple-element.44), calls=%async_computation.2 | async-start | bytes 655360 | tf_op jit(solution)/shard_map/all_to_all | solution.py:35
  87.9 0.7 copy-start.9
  105.5 16.5 %all-to-all-start.4 = ((bf16[32,40,128]{2,1,0:T(8,128)(2,1)}), bf16[32,40,128]{2,1,0:T(8,128)(2,1)S(1)}, u32[]{:S(2)}, u32[]{:S(2)}) async-start(bf16[32,40,128]{2,1,0:T(8,128)(2,1)} %sum_depth.1), calls=%async_computation.4 | async-start | bytes 655360 | tf_op jit(solution)/shard_map/all_to_all | solution.py:35

commit v4 on v3

--- a/solution.py
+++ b/solution.py
@@ -149,8 +149,7 @@
 
 
 def gradient_kernel(
-    gathered, above, below, cot, pw, gain, depth_mid, depth_edge, proj_mid, proj_edge, act,
-    send, grad_gain, grad_shift, gmap, own_depth, gproj, point, slots,
+    gathered, above, below, cot, pw, gain, proj_mid, proj_edge, grad_gain, grad_shift, gproj, gmap
 ):
     n, end = 2 * WIDTH, HEIGHT * WIDTH
     stats = jnp.sum(gathered[...], axis=0)
@@ -159,9 +158,9 @@
     inv_std = 1.0 / jnp.sqrt(variance + 1e-05)
     shift = stats[2:3]
     gained = inv_std * (stats[3:4] - mean * shift)
-    grad_gain[...] = gained
-    grad_shift[...] = shift
-    scale = gain[...] * inv_std
+    grad_gain[...] = gained.reshape(CH)
+    grad_shift[...] = shift.reshape(CH)
+    scale = gain[...].reshape(1, CH) * inv_std
     by_proj = -(scale * inv_std * gained) / COUNT
     offset = -(scale * shift) / COUNT
 
@@ -174,12 +173,18 @@
     gproj[n:end] = gradient(mid_cot, proj_mid[...])
     gproj[end : end + WIDTH] = gradient(cot[0, HEIGHT - 1], proj_edge[n : n + WIDTH])
     gproj[end + WIDTH : end + n] = gradient(below[n : n + WIDTH], proj_edge[n + WIDTH : 2 * n])
+    gmap[...] = lax.dot_general(
+        gproj[...], pw[...], (((1,), (1,)), ((), ())), preferred_element_type=f32
+    ).astype(bf16)
+
+
+def weight_kernel(
+    above, below, depth_mid, depth_edge, gproj, gmap, act, send, own_depth, point, slots
+):
+    n, end = 2 * WIDTH, HEIGHT * WIDTH
     own_depth[0:WIDTH] = depth_edge[WIDTH:n]
     own_depth[WIDTH : end - WIDTH] = depth_mid[...]
     own_depth[end - WIDTH : end] = depth_edge[n : n + WIDTH]
-    gmap[...] = lax.dot_general(
-        gproj[...], pw[...], (((1,), (1,)), ((), ())), preferred_element_type=f32
-    ).astype(bf16)
     whole_point = lax.dot_general(
         own_depth[...], gproj[WIDTH : end + WIDTH], (((0,), (0,)), ((), ())),
         preferred_element_type=f32,
@@ -344,26 +349,27 @@
         grid=(1,),
     )(above, below, partial, act, cotangent, cotangent, depth_weight, point_weight, mid)
     (stats,) = call(total_kernel, "statistics", [((16, 4, CH), f32)])(exchange(stats, PLANE))
-    send, grad_gain, grad_shift, gmap = call(
+    rows = (((HEIGHT + 2) * WIDTH, CH), bf16)
+    grad_gain, grad_shift, gproj, gmap = call(
         gradient_kernel,
         "gradient",
-        [
-            ((32, SLOT, LANES), bf16),
-            ((1, CH), f32),
-            ((1, CH), f32),
-            (((HEIGHT + 2) * WIDTH, CH), bf16),
-        ],
+        [((CH,), f32), ((CH,), f32), rows, rows],
+        in_specs=[VMEM] * 8,
+    )(
+        exchange(stats, DEPTH), above, below, cotangent, point_weight, norm_gain, proj_mid,
+        proj_edge,
+    )
+    (send,) = call(
+        weight_kernel,
+        "weights",
+        [((32, SLOT, LANES), bf16)],
         [
             ((HEIGHT * WIDTH, CH), bf16),
-            (((HEIGHT + 2) * WIDTH, CH), bf16),
             ((3 * CH, LANES), f32),
             ((32, SLOT, LANES), f32),
         ],
-        [VMEM] * 11,
-    )(
-        exchange(stats, DEPTH), above, below, cotangent, point_weight, norm_gain.reshape(1, CH),
-        depth_mid, depth_edge, proj_mid, proj_edge, act,
-    )
+        [VMEM] * 7,
+    )(above, below, depth_mid, depth_edge, gproj, gmap, act)
     grad_fine, grad_coarse, merging = call(
         level_kernel,
         "levels",
@@ -389,8 +395,8 @@
         grad_merging.reshape(2),
         grad_depth,
         grad_point,
-        grad_gain.reshape(CH),
-        grad_shift.reshape(CH),
+        grad_gain,
+        grad_shift,
     )
 
 

time: 123 us -> 121 us (0.984)
  blocking collectives: 32.2 us -> 68.7 us
  waiting for transfers between devices: 40 us -> 20.4 us
  starting transfers between devices: 32.2 us -> 16.9 us
  local copies, waits for them, and re-layouts: 3.62 us -> 1.94 us
    all_to_all x2 -> x4, blocking collectives: 32.2 us -> 68.7 us  [exchange(): return lax.all_to_all(parts, AXES, 0, 0, axis_index_groups=groups)]
    all_to_all x3 -> x1, waiting for transfers between devices: 26.4 us -> 5.93 us  [exchange(): return lax.all_to_all(parts, AXES, 0, 0, axis_index_groups=groups)]
    all_to_all x3 -> x1, starting transfers between devices: 21.2 us -> 5.96 us  [exchange(): return lax.all_to_all(parts, AXES, 0, 0, axis_index_groups=groups)]
    unnamed x22, local copies, waits for them, and re-layouts: 3.62 us -> 1.94 us
    pallas_call x1 -> x2, Pallas kernels: 2.34 us -> 3.23 us  [the longest x1 2.15 us: on_device(): call(weight_kernel, 'weights', [((32, SLOT, LANES), bf16)], [((HEIGHT * W...]
  transfers between devices with their start and end apart: 5 -> 3, of which waited for: 4 -> 2; matrix products, arithmetic and copies ran while one was open for 1% -> 0% of each run, Pallas kernels for 5% -> 5%
where the time goes in v4:
time: 121 us
  blocking collectives  68.7 us (57%)
  waiting for transfers between devices  20.4 us (17%)
  starting transfers between devices  16.9 us (14%)
  Pallas kernels  12.3 us (10%)
  local copies, waits for them, and re-layouts  1.94 us (2%)
    all_to_all x4, blocking collectives, exchange(): return lax.all_to_all(parts, AXES, 0, 0, axis_index_groups=groups)  68.7 us
    ppermute x1, waiting for transfers between devices, on_device(): below = lax.ppermute(head, 'rows', [(i + 1, i) for i in range(n - 1)])  14.5 us
    ppermute x1, starting transfers between devices, on_device(): above = lax.ppermute(tail, 'rows', [(i, i + 1) for i in range(n - 1)])  9.64 us
    all_to_all x1, starting transfers between devices, exchange(): return lax.all_to_all(parts, AXES, 0, 0, axis_index_groups=groups)  5.96 us
    all_to_all x1, waiting for transfers between devices, exchange(): return lax.all_to_all(parts, AXES, 0, 0, axis_index_groups=groups)  5.93 us
    pallas_call x1, Pallas kernels, on_device(): call(level_kernel, 'levels', [(fine_level.shape, bf16), (coarse_level.sha...  3.69 us
  transfers between devices with their start and end apart: 3, of which 2 were waited for; matrix products, arithmetic and copies ran while one was open for 0% of the time, Pallas kernels for 5%

profile of v4, /device:TPU:1, one launch (start us, length us, event | category | flops | bytes accessed | tf_op | source)
XLA Modules:
  0.0 121.0 jit_solution(4688467283271638683)
XLA Ops:
  0.6 0.0 copy-start
  0.6 0.0 copy-start.8
  0.7 0.0 copy-start.5
  0.7 0.0 copy-start.1
  0.7 0.0 copy-start.2
  0.7 0.0 copy-start.7
  0.7 1.9 %pack.1 = (bf16[144,384]{1,0:T(8,128)(2,1)}, bf16[144,384]{1,0:T(8,128)(2,1)}) custom-call(f32[2]{0:T(128)} %mw.5, bf16[1,12,48,384]{3,2,1,0:T(8,128)(2,1)} %fine.1, bf16[1,12,48,384]{3,2,1,0:T(8,128)(2,1)} %fine.1, bf16[1,6,24,384]{3,2,1,0:T(8,128)(2,1)} %coarse.1, bf16[1,6,24,384]{3,2,1,0:T(8,128)(2,1)} %coarse.1, bf16[1,12,48,384]{3,2,1,0:T(8,128)(2,1)} %cot.3, ...), custom_call_target="tpu_custom_call" | custom-call | bytes 1048576 | tf_op jit(solution)/shard_map/pack/pallas_call | solution.py:315
  2.6 9.6 %collective-permute-start = (bf16[144,384]{1,0:T(8,128)(2,1)}, bf16[144,384]{1,0:T(8,128)(2,1)S(1)}, u32[]{:S(2)}, u32[]{:S(2)}) collective-permute-start(bf16[144,384]{1,0:T(8,128)(2,1)} %get-tuple-element.29), channel_id=1, source_target_pairs={{0,1},{1,2},{2,3},{3,4},{4,5},{5,6},{6,7},{7,8},{8,9},{9,10},{10,1... | collective-permute-start | bytes 331784 | tf_op jit(solution)/shard_map/ppermute | solution.py:324
  12.2 1.3 %collective-permute-start.1 = (bf16[144,384]{1,0:T(8,128)(2,1)}, bf16[144,384]{1,0:T(8,128)(2,1)S(1)}, u32[]{:S(2)}, u32[]{:S(2)}) collective-permute-start(bf16[144,384]{1,0:T(8,128)(2,1)} %get-tuple-element.30), channel_id=1, source_target_pairs={{1,0},{2,1},{3,2},{4,3},{5,4},{6,5},{7,6},{8,7},{9,8},{10,9},{11,1... | collective-permute-start | bytes 331784 | tf_op jit(solution)/shard_map/ppermute | solution.py:325
  13.5 0.0 copy-done
  13.5 0.0 copy-done.8
  13.6 0.0 copy-done.5
  13.6 0.0 copy-done.1
  13.6 2.1 %middle.1 = (bf16[480,384]{1,0:T(8,128)(2,1)S(1)}, f32[480,384]{1,0:T(8,128)S(1)}, f32[4,384]{1,0:T(4,128)S(1)}, f32[2,48,384]{2,1,0:T(8,128)S(1)}, f32[12,48,38...) custom-call(f32[2]{0:T(128)S(1)} %copy-done.8, bf16[1,12,48,384]{3,2,1,0:T(8,128)(2,1)S(1)} %copy-done.1, ...), custom_call_target="tpu_custom_call" | custom-call | flops 268435456 | bytes 1048576 | tf_op jit(solution)/shard_map/middle/pallas_call | solution.py:327
  15.7 0.0 copy-start.4
  15.7 1.2 %copy-done.4 = f32[2,12,48,384]{3,2,1,0:T(8,128)} copy-done((f32[2,12,48,384]{3,2,1,0:T(8,128)}, f32[2,12,48,384]{3,2,1,0:T(8,128)S(1)}, u32[]{:S(2)}) %copy-start.4) | copy-done | bytes 1769496
  16.9 0.0 collective-permute-done.above
  16.9 14.5 %collective-permute-done.1.below = bf16[144,384]{1,0:T(8,128)(2,1)S(1)} collective-permute-done((bf16[144,384]{1,0:T(8,128)(2,1)}, bf16[144,384]{1,0:T(8,128)(2,1)S(1)}, u32[]{:S(2)}, u32[]{:S(2)}) %collective-permute-start.1) | collective-permute-done | bytes 110624 | tf_op jit(solution)/shard_map/ppermute | solution.py:325
  31.4 0.4 edge.1
  31.8 16.2 %all_to_all.25.parts = f32[32,4,384]{2,1,0:T(4,128)S(1)} all-to-all(f32[32,4,384]{2,1,0:T(4,128)S(1)} %get-tuple-element.34), channel_id=1, replica_groups={{0,4,8,12,16,20,24,28,32,36,40,44,48,52,56,60,64,68,72,76,80,84,88,92,9..., dimensions={0} | all-to-all | bytes 393216 | tf_op jit(solution)/shard_map/all_to_all | solution.py:35
  48.0 0.1 statistics.1
  48.1 20.3 %all_to_all.26.gathered = f32[16,4,384]{2,1,0:T(4,128)S(1)} all-to-all(f32[16,4,384]{2,1,0:T(4,128)S(1)} %statistics.1), channel_id=1, replica_groups={{0,1,2,3,128,129,130,131,256,257,258,259,384,385,386,387},{4,5,6,7,132,..., dimensions={0} | all-to-all | bytes 196608 | tf_op jit(solution)/shard_map/all_to_all | solution.py:35
  68.4 1.1 gradient.1
  69.5 2.2 %weights.1 = bf16[32,40,128]{2,1,0:T(8,128)(2,1)} custom-call(bf16[144,384]{1,0:T(8,128)(2,1)S(1)} %collective-permute-done.above, bf16[144,384]{1,0:T(8,128)(2,1)S(1)} %collective-permute-done.1.below, bf16[480,384]{1,0:T(8,128)(2,1)S(1)} %get-tuple-element.42.depth_mid, bf16[192,384]{1,0:T(8,128)(2,1)S(1)} %get-tuple-element.43.depth_edge, ...), custom_call_target="tpu_custom_call" | custom-call | bytes 1048576 | tf_op jit(solution)/shard_map/weights/pallas_call | solution.py:362
  71.6 6.0 %all-to-all-start.2 = ((bf16[32,40,128]{2,1,0:T(8,128)(2,1)}), bf16[32,40,128]{2,1,0:T(8,128)(2,1)S(1)}, u32[]{:S(2)}, u32[]{:S(2)}) async-start(bf16[32,40,128]{2,1,0:T(8,128)(2,1)} %weights.1), calls=%async_computation.2 | async-start | bytes 655360 | tf_op jit(solution)/shard_map/all_to_all | solution.py:35
  77.6 3.7 %levels.1 = (bf16[1,12,48,384]{3,2,1,0:T(8,128)(2,1)}, bf16[1,6,24,384]{3,2,1,0:T(8,128)(2,1)}, f32[1,128]{1,0:T(1,128)}) custom-call(f32[2]{0:T(128)} %mw.5, bf16[672,384]{1,0:T(8,128)(2,1)} %copy-done.3, f32[12,48,384]{2,1,0:T(8,128)} %copy-done.6, f32[2,12,48,384]{3,2,1,0:T(8,128)} %copy-done.4, f32[3,3,384]{2,1,0:T(4,128)} %dw.5), custom_call_target="tpu_custom_call" | custom-call | flops 268435456 | bytes 1048576 | tf_op jit(solution)/shard_map/levels/pallas_call | solution.py:373
  81.3 5.9 %all-to-all-done.2.parts = bf16[32,40,128]{2,1,0:T(8,128)(2,1)S(1)} async-done(((bf16[32,40,128]{2,1,0:T(8,128)(2,1)}), bf16[32,40,128]{2,1,0:T(8,128)(2,1)S(1)}, u32[]{:S(2)}, u32[]{:S(2)}) %all-to-all-start.2) | async-done | bytes 327712 | tf_op jit(solution)/shard_map/all_to_all | solution.py:35
  87.2 0.7 copy-done.10
  87.9 0.1 sum_plane.1
  87.9 16.1 %all_to_all.27.parts = bf16[16,40,128]{2,1,0:T(8,128)(2,1)S(1)} all-to-all(bf16[16,40,128]{2,1,0:T(8,128)(2,1)S(1)} %sum_plane.1), channel_id=1, replica_groups={{0,1,2,3,128,129,130,131,256,257,258,259,384,385,386,387},{4,5,6,7,132,..., dimensions={0} | all-to-all | bytes 327680 | tf_op jit(solution)/shard_map/all_to_all | solution.py:35
  104.0 16.2 %all_to_all.28.parts = bf16[32,40,128]{2,1,0:T(8,128)(2,1)S(1)} all-to-all(bf16[32,40,128]{2,1,0:T(8,128)(2,1)S(1)} %sum_depth.1), channel_id=1, replica_groups={{0,4,8,12,16,20,24,28,32,36,40,44,48,52,56,60,64,68,72,76,80,84,88,92,9..., dimensions={0} | all-to-all | bytes 655360 | tf_op jit(solution)/shard_map/all_to_all | solution.py:35
  120.2 0.8 finish.1
  (10 shorter events, 0.1 us)
Async XLA Ops:
  0.6 12.9 %copy-start = (bf16[1,12,48,384]{3,2,1,0:T(8,128)(2,1)S(1)}, bf16[1,12,48,384]{3,2,1,0:T(8,128)(2,1)}, u32[]{:S(2)}) copy-start(bf16[1,12,48,384]{3,2,1,0:T(8,128)(2,1)} %cot.3) | copy-start | bytes 1327108
  0.6 12.9 %copy-start.8 = (f32[2]{0:T(128)S(1)}, f32[2]{0:T(128)}, u32[]{:S(2)}) copy-start(f32[2]{0:T(128)} %mw.5) | copy-start | bytes 28
  0.7 12.9 %copy-start.5 = (bf16[1,6,24,384]{3,2,1,0:T(8,128)(2,1)S(1)}, bf16[1,6,24,384]{3,2,1,0:T(8,128)(2,1)}, u32[]{:S(2)}) copy-start(bf16[1,6,24,384]{3,2,1,0:T(8,128)(2,1)} %coarse.1) | copy-start | bytes 331780
  0.7 12.9 %copy-start.1 = (bf16[1,12,48,384]{3,2,1,0:T(8,128)(2,1)S(1)}, bf16[1,12,48,384]{3,2,1,0:T(8,128)(2,1)}, u32[]{:S(2)}) copy-start(bf16[1,12,48,384]{3,2,1,0:T(8,128)(2,1)} %fine.1) | copy-start | bytes 1327108
  0.7 12.9 %copy-start.2 = (bf16[384,384]{1,0:T(8,128)(2,1)S(1)}, bf16[384,384]{1,0:T(8,128)(2,1)}, u32[]{:S(2)}) copy-start(bf16[384,384]{1,0:T(8,128)(2,1)} %pw.5) | copy-start | bytes 884740
  0.7 12.9 %copy-start.7 = (f32[3,3,384]{2,1,0:T(4,128)S(1)}, f32[3,3,384]{2,1,0:T(4,128)}, u32[]{:S(2)}) copy-start(f32[3,3,384]{2,1,0:T(4,128)} %dw.5) | copy-start | bytes 41476
  2.6 14.4 %collective-permute-start = (bf16[144,384]{1,0:T(8,128)(2,1)}, bf16[144,384]{1,0:T(8,128)(2,1)S(1)}, u32[]{:S(2)}, u32[]{:S(2)}) collective-permute-start(bf16[144,384]{1,0:T(8,128)(2,1)} %get-tuple-element.29), channel_id=1, source_target_pairs={{0,1},{1,2},{2,3},{3,4},{4,5},{5,6},{6,7},{7,8},{8,9},{9,10},{10,1... | collective-permute-start | bytes 331784 | tf_op jit(solution)/shard_map/ppermute | solution.py:324
  12.2 19.2 %collective-permute-start.1 = (bf16[144,384]{1,0:T(8,128)(2,1)}, bf16[144,384]{1,0:T(8,128)(2,1)S(1)}, u32[]{:S(2)}, u32[]{:S(2)}) collective-permute-start(bf16[144,384]{1,0:T(8,128)(2,1)} %get-tuple-element.30), channel_id=1, source_target_pairs={{1,0},{2,1},{3,2},{4,3},{5,4},{6,5},{7,6},{8,7},{9,8},{10,9},{11,1... | collective-permute-start | bytes 331784 | tf_op jit(solution)/shard_map/ppermute | solution.py:325
  15.7 1.2 %copy-start.4 = (f32[2,12,48,384]{3,2,1,0:T(8,128)}, f32[2,12,48,384]{3,2,1,0:T(8,128)S(1)}, u32[]{:S(2)}) copy-start(f32[2,12,48,384]{3,2,1,0:T(8,128)S(1)} %get-tuple-element.39.factor) | copy-start | bytes 5308420
  16.9 52.5 %copy-start.6 = (f32[12,48,384]{2,1,0:T(8,128)}, f32[12,48,384]{2,1,0:T(8,128)S(1)}, u32[]{:S(2)}) copy-start(f32[12,48,384]{2,1,0:T(8,128)S(1)} %get-tuple-element.38.slope) | copy-start | bytes 2654212
  16.9 51.4 %copy-start.9 = (f32[384]{0:T(512)S(1)}, f32[384]{0:T(512)}, u32[]{:S(2)}) copy-start(f32[384]{0:T(512)} %gain.1) | copy-start | bytes 4612
  69.5 2.2 %copy-start.3 = (bf16[672,384]{1,0:T(8,128)(2,1)}, bf16[672,384]{1,0:T(8,128)(2,1)S(1)}, u32[]{:S(2)}) copy-start(bf16[672,384]{1,0:T(8,128)(2,1)S(1)} %get-tuple-element.37.gmap) | copy-start | bytes 1548292
  71.6 15.6 %all-to-all-start.2 = ((bf16[32,40,128]{2,1,0:T(8,128)(2,1)}), bf16[32,40,128]{2,1,0:T(8,128)(2,1)S(1)}, u32[]{:S(2)}, u32[]{:S(2)}) async-start(bf16[32,40,128]{2,1,0:T(8,128)(2,1)} %weights.1), calls=%async_computation.2 | async-start | bytes 655360 | tf_op jit(solution)/shard_map/all_to_all | solution.py:35
  87.2 0.7 copy-start.10

commit v5 on v4

--- a/solution.py
+++ b/solution.py
@@ -96,14 +96,20 @@
         out[2 * WIDTH : 3 * WIDTH] = cot[0, 0]
 
 
+def inside():
+    place, end = lax.axis_index("rows"), lax.axis_size("rows") - 1
+    return {0: jnp.where(place == 0, 0.0, 1.0), HEIGHT + 1: jnp.where(place == end, 0.0, 1.0)}
+
+
 def factors(row, up, share):
     merged, sig, act = activate(row, up, share)
     slope = sig * (1.0 + merged * (1.0 - sig))
-    return act, slope, ((row - merged) / share[2], (up - merged) / share[2])
+    scaled = slope / share[2]
+    return act, slope, (scaled * (row - merged), scaled * (up - merged))
 
 
 def middle_kernel(
-    mw, fine, coarse, dw, pw, cot, depth, proj, stats, partial, act, factor, slope, up
+    mw, fine, coarse, dw, pw, cot, depth, proj, stats, partial, act, weigh, slope, up, factor
 ):
     share = shares(mw)
     up[...] = doubled(coarse[0].reshape(-1, CH))
@@ -120,6 +126,11 @@
                 depth[(i - 1) * WIDTH : i * WIDTH, c] = sums.astype(bf16)
             else:
                 partial[i // last, :, c] = sums
+        for i in range(-1, HEIGHT + 1):
+            taps = [a for a in range(3) if 0 <= i + a - 1 <= last]
+            for t in range(2):
+                rows = [factor[t, i + a - 1, :, c] for a in taps]
+                weigh[t, i + 1, :, c] = convolve(rows, taps, dw, c)
     proj[...] = jnp.dot(depth[...], pw[...], preferred_element_type=f32)
     own = cot[0, 1:last].reshape(-1, CH).astype(f32)
     for k, s in enumerate(statistics(proj[...], own)):
@@ -179,7 +190,7 @@
 
 
 def weight_kernel(
-    above, below, depth_mid, depth_edge, gproj, gmap, act, send, own_depth, point, slots
+    above, below, depth_mid, depth_edge, gproj, gmap, act, weigh, send, own_depth, point, slots
 ):
     n, end = 2 * WIDTH, HEIGHT * WIDTH
     own_depth[0:WIDTH] = depth_edge[WIDTH:n]
@@ -191,12 +202,19 @@
     )
     zero = jnp.zeros((1, LANES), f32)
     small = [zero] * 32
+    by_weight = [jnp.zeros((8, LANES), f32)] * 2
+    keep = inside()
     for k, c in enumerate(blocks()):
         point[k * CH : (k + 1) * CH] = whole_point[:, c]
         taps = [jnp.zeros((8, LANES), f32)] * 9
         ends = [halo[0:WIDTH, c].astype(f32) for halo in (above, below)]
-        for i in range(HEIGHT):
+        for i in range(-1, HEIGHT + 1):
             x = gmap[(i + 1) * WIDTH : (i + 2) * WIDTH, c].astype(f32)
+            x = x * keep[i + 1] if i + 1 in keep else x
+            for t in range(2):
+                by_weight[t] = by_weight[t] + folded(weigh[t, i + 1, :, c] * x)
+            if i + 1 in keep:
+                continue
             moved = from_right(x), x, from_left(x)
             for a in range(3):
                 r = i + a - 1
@@ -205,6 +223,8 @@
                     taps[3 * a + b] = taps[3 * a + b] + folded(row * moved[b])
         for t in range(9):
             small[3 * t + k] = jnp.sum(taps[t], axis=0, keepdims=True)
+    for t in range(2):
+        small[27 + t] = jnp.sum(by_weight[t], axis=0, keepdims=True)
     for s in range(32):
         slots[s, 0:PIECE] = point[s * PIECE : (s + 1) * PIECE]
         high = small[s].astype(bf16).astype(f32)
@@ -212,17 +232,10 @@
     send[...] = slots[...].astype(bf16)
 
 
-def level_kernel(
-    mw, gmap, slope, factor, dw, grad_fine, grad_coarse, merging, moved, pairs
-):
+def level_kernel(mw, gmap, slope, dw, grad_fine, grad_coarse, moved, pairs):
     share = shares(mw)
     m = HEIGHT * HALF // 2
-    place = lax.axis_index("rows")
-    keep = {
-        0: jnp.where(place == 0, 0.0, 1.0),
-        HEIGHT + 1: jnp.where(place == lax.axis_size("rows") - 1, 0.0, 1.0),
-    }
-    by_weight = [jnp.zeros((8, LANES), f32)] * 2
+    keep = inside()
     for k, c in enumerate(blocks()):
         for r in range(HEIGHT + 2):
             x = gmap[r * WIDTH : (r + 1) * WIDTH, c].astype(f32)
@@ -236,8 +249,6 @@
                 for b in range(3):
                     grad_act = grad_act + moved[b, p + 2 - a, :, c] * dw[a, b : b + 1, c]
             grad_merged = grad_act * slope[p, :, c]
-            for t in range(2):
-                by_weight[t] = by_weight[t] + folded(grad_merged * factor[t, p, :, c])
             grad_fine[0, p, :, c] = (grad_merged * share[0]).astype(bf16)
             at = 2 * k * m + (p // 2) * WIDTH
             if p % 2 == 0:
@@ -246,38 +257,29 @@
                 pairs[at : at + WIDTH] = pairs[at : at + WIDTH] + grad_merged
         both = pairs[pl.ds(2 * k * m, m, stride=2)] + pairs[pl.ds(2 * k * m + 1, m, stride=2)]
         grad_coarse[0, :, :, c] = (both * share[1]).astype(bf16).reshape(HEIGHT // 2, HALF, LANES)
-    lane = lax.broadcasted_iota(jnp.int32, (1, LANES), 1)
-    first, second = [
-        jnp.sum(jnp.sum(x, axis=0, keepdims=True), axis=1, keepdims=True) for x in by_weight
-    ]
-    merging[...] = jnp.where(lane == 0, first, jnp.where(lane == 1, second, 0.0))
-
-
-def relay_kernel(parts, *refs):
-    out = refs[-1]
+
+
+def relay_kernel(parts, out):
     total = jnp.sum(parts[...].astype(f32), axis=0)
+    value = total[PIECE : PIECE + 1] + total[PIECE + 1 : PIECE + 2]
+    high = value.astype(bf16).astype(f32)
     row = lax.broadcasted_iota(jnp.int32, (SLOT, LANES), 0)
-    for at in (PIECE, PIECE + 2):
-        value = total[at : at + 1] + total[at + 1 : at + 2]
-        if at > PIECE and len(refs) > 1:
-            value = refs[0][...]
-        high = value.astype(bf16).astype(f32)
-        total = jnp.where(row == at, high, jnp.where(row == at + 1, value - high, total))
+    total = jnp.where(row == PIECE, high, jnp.where(row == PIECE + 1, value - high, total))
     out[...] = jnp.broadcast_to(total.astype(bf16)[None], out.shape)
 
 
 def finish_kernel(parts, grad_point, grad_depth, grad_merging, point):
-    rest, merging = [], jnp.zeros((1, LANES), f32)
+    rest = []
     for s in range(32):
         slot = parts[s].astype(f32)
         point[s * PIECE : (s + 1) * PIECE] = slot[0:PIECE]
         rest.append(slot[PIECE : PIECE + 1] + slot[PIECE + 1 : PIECE + 2])
-        merging = merging + (slot[PIECE + 2 : PIECE + 3] + slot[PIECE + 3 : PIECE + 4])
     for k, c in enumerate(blocks()):
         grad_point[:, c] = point[k * CH : (k + 1) * CH].astype(bf16)
         for t in range(9):
             grad_depth[t // 3, t % 3 : t % 3 + 1, c] = rest[3 * t + k]
-    grad_merging[...] = merging[:, 0:2]
+    sums = [jnp.sum(rest[27 + t], axis=1, keepdims=True) for t in range(2)]
+    grad_merging[...] = jnp.concatenate(sums, axis=1)
 
 
 VMEM = pl.BlockSpec(memory_space=pltpu.VMEM)
@@ -324,7 +326,7 @@
     above = lax.ppermute(tail, "rows", [(i, i + 1) for i in range(n - 1)])
     below = lax.ppermute(head, "rows", [(i + 1, i) for i in range(n - 1)])
     whole = ((HEIGHT, WIDTH, CH), f32)
-    depth_mid, proj_mid, mid, partial, act, factor, slope = call(
+    depth_mid, proj_mid, mid, partial, act, weigh, slope = call(
         middle_kernel,
         "middle",
         [
@@ -333,10 +335,10 @@
             ((4, CH), f32),
             ((2, WIDTH, CH), f32),
             whole,
-            ((2,) + whole[0], f32),
+            ((2, HEIGHT + 2, WIDTH, CH), f32),
             whole,
         ],
-        [((HEIGHT * HALF, CH), f32)],
+        [((HEIGHT * HALF, CH), f32), ((2,) + whole[0], f32)],
         [SMEM] + [VMEM] * 5,
         cost=1 << 28,
     )(merging_weights, fine_level, coarse_level, depth_weight, point_weight, cotangent)
@@ -368,20 +370,18 @@
             ((3 * CH, LANES), f32),
             ((32, SLOT, LANES), f32),
         ],
-        [VMEM] * 7,
-    )(above, below, depth_mid, depth_edge, gproj, gmap, act)
-    grad_fine, grad_coarse, merging = call(
+        [VMEM] * 8,
+    )(above, below, depth_mid, depth_edge, gproj, gmap, act, weigh)
+    grad_fine, grad_coarse = call(
         level_kernel,
         "levels",
-        [(fine_level.shape, bf16), (coarse_level.shape, bf16), ((1, LANES), f32)],
+        [(fine_level.shape, bf16), (coarse_level.shape, bf16)],
         [((3, HEIGHT + 2, WIDTH, CH), f32), ((3 * HEIGHT * HALF, LANES), f32)],
-        [SMEM] + [VMEM] * 4,
+        [SMEM] + [VMEM] * 3,
         cost=1 << 28,
         limit=56,
-    )(merging_weights, gmap, slope, factor, depth_weight)
-    (part,) = call(
-        relay_kernel, "sum_plane", [((16, SLOT, LANES), bf16)], in_specs=[VMEM] * 2
-    )(exchange(send, PLANE), merging)
+    )(merging_weights, gmap, slope, depth_weight)
+    (part,) = call(relay_kernel, "sum_plane", [((16, SLOT, LANES), bf16)])(exchange(send, PLANE))
     (part,) = call(relay_kernel, "sum_depth", [((32, SLOT, LANES), bf16)])(exchange(part, DEPTH))
     grad_point, grad_depth, grad_merging = call(
         finish_kernel,

time: 121 us -> 121 us (level)
  blocking collectives: 68.7 us -> 67.4 us
    ppermute x1, waiting for transfers between devices: 14.5 us -> 12.8 us  [on_device(): below = lax.ppermute(head, 'rows', [(i + 1, i) for i in range(n - 1)])]
    pallas_call x1, Pallas kernels: 2.08 us -> 3.64 us  [on_device(): call(middle_kernel, 'middle', [((MID * WIDTH, CH), bf16), ((MID * WIDTH,...]
    all_to_all x4, blocking collectives: 68.7 us -> 67.4 us  [exchange(): return lax.all_to_all(parts, AXES, 0, 0, axis_index_groups=groups)]
where the time goes in v5:
time: 121 us; the launch traced here: 120 us
  blocking collectives  67.4 us (56%)
  waiting for transfers between devices  19.5 us (16%)
  starting transfers between devices  17.8 us (15%)
  Pallas kernels  13.3 us (11%)
  local copies, waits for them, and re-layouts  1.4 us (1%)
    all_to_all x4, blocking collectives, exchange(): return lax.all_to_all(parts, AXES, 0, 0, axis_index_groups=groups)  67.4 us
    ppermute x1, waiting for transfers between devices, on_device(): below = lax.ppermute(head, 'rows', [(i + 1, i) for i in range(n - 1)])  12.8 us
    ppermute x1, starting transfers between devices, on_device(): above = lax.ppermute(tail, 'rows', [(i, i + 1) for i in range(n - 1)])  9.64 us
    all_to_all x1, starting transfers between devices, exchange(): return lax.all_to_all(parts, AXES, 0, 0, axis_index_groups=groups)  6.88 us
    all_to_all x1, waiting for transfers between devices, exchange(): return lax.all_to_all(parts, AXES, 0, 0, axis_index_groups=groups)  6.69 us
    pallas_call x1, Pallas kernels, on_device(): call(middle_kernel, 'middle', [((MID * WIDTH, CH), bf16), ((MID * WIDTH,...  3.64 us
    pallas_call x1, Pallas kernels, on_device(): call(level_kernel, 'levels', [(fine_level.shape, bf16), (coarse_level.sha...  2.93 us
  transfers between devices with their start and end apart: 3, of which 2 were waited for; matrix products, arithmetic and copies ran while one was open for 0% of the time, Pallas kernels for 5%

profile of v5, /device:TPU:1, one launch (start us, length us, event | category | flops | bytes accessed | tf_op | source)
XLA Modules:
  0.0 120.1 jit_solution(6054010508641507388)
XLA Ops:
  0.6 0.0 copy-start
  0.6 0.0 copy-start.4
  0.7 0.0 copy-start.1
  0.7 0.0 copy-start.2
  0.7 1.9 %pack.1 = (bf16[144,384]{1,0:T(8,128)(2,1)}, bf16[144,384]{1,0:T(8,128)(2,1)}) custom-call(f32[2]{0:T(128)} %mw.5, bf16[1,12,48,384]{3,2,1,0:T(8,128)(2,1)} %fine.1, bf16[1,12,48,384]{3,2,1,0:T(8,128)(2,1)} %fine.1, bf16[1,6,24,384]{3,2,1,0:T(8,128)(2,1)} %coarse.1, bf16[1,6,24,384]{3,2,1,0:T(8,128)(2,1)} %coarse.1, bf16[1,12,48,384]{3,2,1,0:T(8,128)(2,1)} %cot.3, ...), custom_call_target="tpu_custom_call" | custom-call | bytes 1048576 | tf_op jit(solution)/shard_map/pack/pallas_call | solution.py:317
  2.6 9.6 %collective-permute-start = (bf16[144,384]{1,0:T(8,128)(2,1)}, bf16[144,384]{1,0:T(8,128)(2,1)S(1)}, u32[]{:S(2)}, u32[]{:S(2)}) collective-permute-start(bf16[144,384]{1,0:T(8,128)(2,1)} %get-tuple-element.28), channel_id=1, source_target_pairs={{0,1},{1,2},{2,3},{3,4},{4,5},{5,6},{6,7},{7,8},{8,9},{9,10},{10,1... | collective-permute-start | bytes 331784 | tf_op jit(solution)/shard_map/ppermute | solution.py:326
  12.2 1.3 %collective-permute-start.1 = (bf16[144,384]{1,0:T(8,128)(2,1)}, bf16[144,384]{1,0:T(8,128)(2,1)S(1)}, u32[]{:S(2)}, u32[]{:S(2)}) collective-permute-start(bf16[144,384]{1,0:T(8,128)(2,1)} %get-tuple-element.29), channel_id=1, source_target_pairs={{1,0},{2,1},{3,2},{4,3},{5,4},{6,5},{7,6},{8,7},{9,8},{10,9},{11,1... | collective-permute-start | bytes 331784 | tf_op jit(solution)/shard_map/ppermute | solution.py:327
  13.5 0.0 copy-done
  13.5 0.0 copy-done.4
  13.5 0.0 copy-done.1
  13.6 0.0 copy-start.6
  13.6 0.7 copy-done.6
  14.3 0.7 copy-done.7
  14.9 3.6 %middle.1 = (bf16[480,384]{1,0:T(8,128)(2,1)S(1)}, f32[480,384]{1,0:T(8,128)S(1)}, f32[4,384]{1,0:T(4,128)S(1)}, f32[2,48,384]{2,1,0:T(8,128)S(1)}, f32[12,48,38...) custom-call(f32[2]{0:T(128)S(1)} %copy-done.7, bf16[1,12,48,384]{3,2,1,0:T(8,128)(2,1)S(1)} %copy-done.1, ...), custom_call_target="tpu_custom_call" | custom-call | flops 268435456 | bytes 1048576 | tf_op jit(solution)/shard_map/middle/pallas_call | solution.py:329
  18.6 0.0 copy-start.5
  18.6 0.0 collective-permute-done.above
  18.6 12.8 %collective-permute-done.1.below = bf16[144,384]{1,0:T(8,128)(2,1)S(1)} collective-permute-done((bf16[144,384]{1,0:T(8,128)(2,1)}, bf16[144,384]{1,0:T(8,128)(2,1)S(1)}, u32[]{:S(2)}, u32[]{:S(2)}) %collective-permute-start.1) | collective-permute-done | bytes 110624 | tf_op jit(solution)/shard_map/ppermute | solution.py:327
  31.4 0.4 edge.1
  31.8 16.2 %all_to_all.25.parts = f32[32,4,384]{2,1,0:T(4,128)S(1)} all-to-all(f32[32,4,384]{2,1,0:T(4,128)S(1)} %get-tuple-element.33), channel_id=1, replica_groups={{0,4,8,12,16,20,24,28,32,36,40,44,48,52,56,60,64,68,72,76,80,84,88,92,9..., dimensions={0} | all-to-all | bytes 393216 | tf_op jit(solution)/shard_map/all_to_all | solution.py:35
  48.0 0.1 statistics.1
  48.0 20.3 %all_to_all.26.gathered = f32[16,4,384]{2,1,0:T(4,128)S(1)} all-to-all(f32[16,4,384]{2,1,0:T(4,128)S(1)} %statistics.1), channel_id=1, replica_groups={{0,1,2,3,128,129,130,131,256,257,258,259,384,385,386,387},{4,5,6,7,132,..., dimensions={0} | all-to-all | bytes 196608 | tf_op jit(solution)/shard_map/all_to_all | solution.py:35
  68.3 1.1 gradient.1
  69.4 1.7 %weights.1 = bf16[32,40,128]{2,1,0:T(8,128)(2,1)S(1)} custom-call(bf16[144,384]{1,0:T(8,128)(2,1)S(1)} %collective-permute-done.above, bf16[144,384]{1,0:T(8,128)(2,1)S(1)} %collective-permute-done.1.below, bf16[480,384]{1,0:T(8,128)(2,1)S(1)} %get-tuple-element.40.depth_mid, bf16[192,384]{1,0:T(8,128)(2,1)S(1)} %get-tuple-element.41.depth_edge, ...), custom_call_target="tpu_custom_call" | custom-call | bytes 1048576 | tf_op jit(solution)/shard_map/weights/pallas_call | solution.py:364
  71.1 0.0 copy-done.3
  71.1 14.8 %all_to_all.27.parts = bf16[32,40,128]{2,1,0:T(8,128)(2,1)S(1)} all-to-all(bf16[32,40,128]{2,1,0:T(8,128)(2,1)S(1)} %weights.1), channel_id=1, replica_groups={{0,4,8,12,16,20,24,28,32,36,40,44,48,52,56,60,64,68,72,76,80,84,88,92,9..., dimensions={0} | all-to-all | bytes 655360 | tf_op jit(solution)/shard_map/all_to_all | solution.py:35
  85.9 0.1 sum_plane.1
  85.9 16.1 %all_to_all.28.parts = bf16[16,40,128]{2,1,0:T(8,128)(2,1)S(1)} all-to-all(bf16[16,40,128]{2,1,0:T(8,128)(2,1)S(1)} %sum_plane.1), channel_id=1, replica_groups={{0,1,2,3,128,129,130,131,256,257,258,259,384,385,386,387},{4,5,6,7,132,..., dimensions={0} | all-to-all | bytes 327680 | tf_op jit(solution)/shard_map/all_to_all | solution.py:35
  102.1 0.8 sum_depth.1
  102.8 6.9 %all-to-all-start.4 = ((bf16[32,40,128]{2,1,0:T(8,128)(2,1)}), bf16[32,40,128]{2,1,0:T(8,128)(2,1)S(1)}, u32[]{:S(2)}, u32[]{:S(2)}) async-start(bf16[32,40,128]{2,1,0:T(8,128)(2,1)} %sum_depth.1), calls=%async_computation.4 | async-start | bytes 655360 | tf_op jit(solution)/shard_map/all_to_all | solution.py:35
  109.7 2.9 %levels.1 = (bf16[1,12,48,384]{3,2,1,0:T(8,128)(2,1)}, bf16[1,6,24,384]{3,2,1,0:T(8,128)(2,1)}) custom-call(f32[2]{0:T(128)} %mw.5, bf16[672,384]{1,0:T(8,128)(2,1)} %copy-done.3, f32[12,48,384]{2,1,0:T(8,128)} %copy-done.5, f32[3,3,384]{2,1,0:T(4,128)} %dw.5), custom_call_target="tpu_custom_call" | custom-call | flops 268435456 | bytes 1048576 | tf_op jit(solution)/shard_map/levels/pallas_call | solution.py:375
  112.6 6.7 %all-to-all-done.4.parts = bf16[32,40,128]{2,1,0:T(8,128)(2,1)S(1)} async-done(((bf16[32,40,128]{2,1,0:T(8,128)(2,1)}), bf16[32,40,128]{2,1,0:T(8,128)(2,1)S(1)}, u32[]{:S(2)}, u32[]{:S(2)}) %all-to-all-start.4) | async-done | bytes 327712 | tf_op jit(solution)/shard_map/all_to_all | solution.py:35
  119.3 0.8 finish.1
  (6 shorter events, 0.0 us)
Async XLA Ops:
  0.6 12.9 %copy-start = (bf16[1,12,48,384]{3,2,1,0:T(8,128)(2,1)S(1)}, bf16[1,12,48,384]{3,2,1,0:T(8,128)(2,1)}, u32[]{:S(2)}) copy-start(bf16[1,12,48,384]{3,2,1,0:T(8,128)(2,1)} %cot.3) | copy-start | bytes 1327108
  0.6 12.9 %copy-start.4 = (bf16[1,6,24,384]{3,2,1,0:T(8,128)(2,1)S(1)}, bf16[1,6,24,384]{3,2,1,0:T(8,128)(2,1)}, u32[]{:S(2)}) copy-start(bf16[1,6,24,384]{3,2,1,0:T(8,128)(2,1)} %coarse.1) | copy-start | bytes 331780
  0.7 12.9 %copy-start.1 = (bf16[1,12,48,384]{3,2,1,0:T(8,128)(2,1)S(1)}, bf16[1,12,48,384]{3,2,1,0:T(8,128)(2,1)}, u32[]{:S(2)}) copy-start(bf16[1,12,48,384]{3,2,1,0:T(8,128)(2,1)} %fine.1) | copy-start | bytes 1327108
  0.7 12.9 %copy-start.2 = (bf16[384,384]{1,0:T(8,128)(2,1)S(1)}, bf16[384,384]{1,0:T(8,128)(2,1)}, u32[]{:S(2)}) copy-start(bf16[384,384]{1,0:T(8,128)(2,1)} %pw.5) | copy-start | bytes 884740
  2.6 16.0 %collective-permute-start = (bf16[144,384]{1,0:T(8,128)(2,1)}, bf16[144,384]{1,0:T(8,128)(2,1)S(1)}, u32[]{:S(2)}, u32[]{:S(2)}) collective-permute-start(bf16[144,384]{1,0:T(8,128)(2,1)} %get-tuple-element.28), channel_id=1, source_target_pairs={{0,1},{1,2},{2,3},{3,4},{4,5},{5,6},{6,7},{7,8},{8,9},{9,10},{10,1... | collective-permute-start | bytes 331784 | tf_op jit(solution)/shard_map/ppermute | solution.py:326
  12.2 19.2 %collective-permute-start.1 = (bf16[144,384]{1,0:T(8,128)(2,1)}, bf16[144,384]{1,0:T(8,128)(2,1)S(1)}, u32[]{:S(2)}, u32[]{:S(2)}) collective-permute-start(bf16[144,384]{1,0:T(8,128)(2,1)} %get-tuple-element.29), channel_id=1, source_target_pairs={{1,0},{2,1},{3,2},{4,3},{5,4},{6,5},{7,6},{8,7},{9,8},{10,9},{11,1... | collective-permute-start | bytes 331784 | tf_op jit(solution)/shard_map/ppermute | solution.py:327
  13.6 0.7 copy-start.6
  14.3 0.7 copy-start.7
  14.9 53.4 %copy-start.8 = (f32[384]{0:T(512)S(1)}, f32[384]{0:T(512)}, u32[]{:S(2)}) copy-start(f32[384]{0:T(512)} %gain.1) | copy-start | bytes 4612
  18.6 50.8 %copy-start.5 = (f32[12,48,384]{2,1,0:T(8,128)}, f32[12,48,384]{2,1,0:T(8,128)S(1)}, u32[]{:S(2)}) copy-start(f32[12,48,384]{2,1,0:T(8,128)S(1)} %get-tuple-element.37.slope) | copy-start | bytes 2654212
  69.4 1.7 %copy-start.3 = (bf16[672,384]{1,0:T(8,128)(2,1)}, bf16[672,384]{1,0:T(8,128)(2,1)S(1)}, u32[]{:S(2)}) copy-start(bf16[672,384]{1,0:T(8,128)(2,1)S(1)} %get-tuple-element.36.gmap) | copy-start | bytes 1548292
  102.8 16.5 %all-to-all-start.4 = ((bf16[32,40,128]{2,1,0:T(8,128)(2,1)}), bf16[32,40,128]{2,1,0:T(8,128)(2,1)S(1)}, u32[]{:S(2)}, u32[]{:S(2)}) async-start(bf16[32,40,128]{2,1,0:T(8,128)(2,1)} %sum_depth.1), calls=%async_computation.4 | async-start | bytes 655360 | tf_op jit(solution)/shard_map/all_to_all | solution.py:35

commit v6 on v5

--- a/solution.py
+++ b/solution.py
@@ -85,15 +85,38 @@
     return [jnp.sum(folded(p), axis=0, keepdims=True) for p in parts]
 
 
-def pack_kernel(mw, ft, fb, ct, cb, gt, gb, head, tail):
+def pack_kernel(mw, fine, coarse, cot, head, tail, fines, coarses, acts, sems):
+    last = HEIGHT - 1
+    ends = ((head, 0, 0, 0, (0, 1)), (tail, last - 1, HEIGHT // 2 - 1, last, (1, 0)))
+    loads, moves = [], []
+    for e, (out, first, low, row, _) in enumerate(ends):
+        loads.append(
+            (
+                pltpu.make_async_copy(fine.at[0, pl.ds(first, 2)], fines.at[e], sems.at[4 * e]),
+                pltpu.make_async_copy(coarse.at[0, low], coarses.at[e], sems.at[4 * e + 1]),
+            )
+        )
+        rows = out.at[pl.ds(2 * WIDTH, WIDTH)]
+        moves.append(pltpu.make_async_copy(cot.at[0, row], rows, sems.at[4 * e + 2]))
+    for pair in loads:
+        for copy in pair:
+            copy.start()
+    for copy in moves:
+        copy.start()
     share = shares(mw)
-    for out, fine, coarse, cot, rows in ((head, ft, ct, gt, (0, 1)), (tail, fb, cb, gb, (1, 0))):
-        up = doubled(coarse[0, 0])
-        for k, r in enumerate(rows):
+    for e, (out, _, _, _, order) in enumerate(ends):
+        for copy in loads[e]:
+            copy.wait()
+        up = doubled(coarses[e])
+        for k, r in enumerate(order):
             for c in blocks():
-                act = activate(fine[0, r, :, c].astype(f32), up[:, c], share)[2]
-                out[k * WIDTH : (k + 1) * WIDTH, c] = act.astype(bf16)
-        out[2 * WIDTH : 3 * WIDTH] = cot[0, 0]
+                act = activate(fines[e, r, :, c].astype(f32), up[:, c], share)[2]
+                acts[e, k * WIDTH : (k + 1) * WIDTH, c] = act.astype(bf16)
+        rows = out.at[pl.ds(0, 2 * WIDTH)]
+        moves.append(pltpu.make_async_copy(acts.at[e], rows, sems.at[4 * e + 3]))
+        moves[-1].start()
+    for copy in moves:
+        copy.wait()
 
 
 def inside():
@@ -313,15 +336,21 @@
 def on_device(
     fine_level, coarse_level, merging_weights, depth_weight, point_weight, norm_gain, cotangent
 ):
-    ends = (fine_level, fine_level, coarse_level, coarse_level, cotangent, cotangent)
-    head, tail = call(
+    any_space = pl.BlockSpec(memory_space=pl.ANY)
+    head, tail = pl.pallas_call(
         pack_kernel,
-        "pack",
-        [((3 * WIDTH, CH), bf16)] * 2,
-        in_specs=[SMEM] + FINE_ENDS + COARSE_ENDS + COT_ENDS,
-        grid=(1,),
-        limit=56,
-    )(merging_weights, *ends)
+        name="pack",
+        out_shape=[jax.ShapeDtypeStruct((3 * WIDTH, CH), bf16)] * 2,
+        in_specs=[SMEM] + [any_space] * 3,
+        out_specs=[any_space] * 2,
+        scratch_shapes=[
+            pltpu.VMEM((2, 2, WIDTH, CH), bf16),
+            pltpu.VMEM((2, HALF, CH), bf16),
+            pltpu.VMEM((2, 2 * WIDTH, CH), bf16),
+            pltpu.SemaphoreType.DMA((8,)),
+        ],
+        compiler_params=pltpu.CompilerParams(vmem_limit_bytes=56 << 20),
+    )(merging_weights, fine_level, coarse_level, cotangent)
     n = lax.axis_size("rows")
     above = lax.ppermute(tail, "rows", [(i, i + 1) for i in range(n - 1)])
     below = lax.ppermute(head, "rows", [(i + 1, i) for i in range(n - 1)])

time: 121 us -> 123 us (1.017)
  local copies, waits for them, and re-layouts: 1.4 us -> 5.28 us
  waiting for transfers between devices: 19.5 us -> 15.7 us
  Pallas kernels: 13.3 us -> 15.6 us
    unnamed x18 -> x22, local copies, waits for them, and re-layouts: 1.4 us -> 5.28 us
    ppermute x1, waiting for transfers between devices: 12.8 us -> 8.96 us  [on_device(): below = lax.ppermute(head, 'rows', [(i + 1, i) for i in range(n - 1)])]
    pallas_call x1, Pallas kernels: 1.9 us -> 4.21 us  [on_device(): pl.pallas_call(pack_kernel, name='pack', out_shape=[jax.ShapeDtypeStruct(...]
where the time goes in v6:
time: 123 us; the launch traced here: 122 us
  blocking collectives  67.4 us (55%)
  starting transfers between devices  17.8 us (14%)
  waiting for transfers between devices  15.7 us (13%)
  Pallas kernels  15.6 us (13%)
  local copies, waits for them, and re-layouts  5.28 us (4%)
    all_to_all x4, blocking collectives, exchange(): return lax.all_to_all(parts, AXES, 0, 0, axis_index_groups=groups)  67.4 us
    ppermute x1, starting transfers between devices, on_device(): above = lax.ppermute(tail, 'rows', [(i, i + 1) for i in range(n - 1)])  9.65 us
    ppermute x1, waiting for transfers between devices, on_device(): below = lax.ppermute(head, 'rows', [(i + 1, i) for i in range(n - 1)])  8.96 us
    all_to_all x1, starting transfers between devices, exchange(): return lax.all_to_all(parts, AXES, 0, 0, axis_index_groups=groups)  6.88 us
    all_to_all x1, waiting for transfers between devices, exchange(): return lax.all_to_all(parts, AXES, 0, 0, axis_index_groups=groups)  6.69 us
    unnamed x22, local copies, waits for them, and re-layouts  5.28 us
    pallas_call x1, Pallas kernels, on_device(): pl.pallas_call(pack_kernel, name='pack', out_shape=[jax.ShapeDtypeStruct(...  4.21 us
    pallas_call x1, Pallas kernels, on_device(): call(middle_kernel, 'middle', [((MID * WIDTH, CH), bf16), ((MID * WIDTH,...  3.62 us
  transfers between devices with their start and end apart: 3, of which 2 were waited for; matrix products, arithmetic and copies ran while one was open for 0% of the time, Pallas kernels for 5%

profile of v6, /device:TPU:1, one launch (start us, length us, event | category | flops | bytes accessed | tf_op | source)
XLA Modules:
  0.0 122.5 jit_solution(16847027842502655052)
XLA Ops:
  0.6 0.0 copy-start.1
  0.6 4.2 %pack.1 = (bf16[144,384]{1,0:T(8,128)(2,1)}, bf16[144,384]{1,0:T(8,128)(2,1)}) custom-call(f32[2]{0:T(128)} %mw.5, bf16[1,12,48,384]{3,2,1,0:T(8,128)(2,1)} %fine.3, bf16[1,6,24,384]{3,2,1,0:T(8,128)(2,1)} %coarse.3, bf16[1,12,48,384]{3,2,1,0:T(8,128)(2,1)} %cot.5), custom_call_target="tpu_custom_call" | custom-call | tf_op jit(solution)/shard_map/pack/pallas_call | solution.py:340
  4.9 9.6 %collective-permute-start = (bf16[144,384]{1,0:T(8,128)(2,1)}, bf16[144,384]{1,0:T(8,128)(2,1)S(1)}, u32[]{:S(2)}, u32[]{:S(2)}) collective-permute-start(bf16[144,384]{1,0:T(8,128)(2,1)} %get-tuple-element.28), channel_id=1, source_target_pairs={{0,1},{1,2},{2,3},{3,4},{4,5},{5,6},{6,7},{7,8},{8,9},{9,10},{10,1... | collective-permute-start | bytes 331784 | tf_op jit(solution)/shard_map/ppermute | solution.py:355
  14.5 1.3 %collective-permute-start.1 = (bf16[144,384]{1,0:T(8,128)(2,1)}, bf16[144,384]{1,0:T(8,128)(2,1)S(1)}, u32[]{:S(2)}, u32[]{:S(2)}) collective-permute-start(bf16[144,384]{1,0:T(8,128)(2,1)} %get-tuple-element.29), channel_id=1, source_target_pairs={{1,0},{2,1},{3,2},{4,3},{5,4},{6,5},{7,6},{8,7},{9,8},{10,9},{11,1... | collective-permute-start | bytes 331784 | tf_op jit(solution)/shard_map/ppermute | solution.py:356
  15.8 0.0 copy-start
  15.8 1.0 copy-done
  16.8 1.0 copy-done.2
  17.8 1.0 copy-done.5
  18.8 0.9 copy-done.7
  19.7 0.7 copy-done.8
  20.4 0.7 copy-done.9
  21.1 3.6 %middle.1 = (bf16[480,384]{1,0:T(8,128)(2,1)S(1)}, f32[480,384]{1,0:T(8,128)S(1)}, f32[4,384]{1,0:T(4,128)S(1)}, f32[2,48,384]{2,1,0:T(8,128)S(1)}, f32[12,48,38...) custom-call(f32[2]{0:T(128)S(1)} %copy-done.9, bf16[1,12,48,384]{3,2,1,0:T(8,128)(2,1)S(1)} %copy-done.5, ...), custom_call_target="tpu_custom_call" | custom-call | flops 268435456 | bytes 1048576 | tf_op jit(solution)/shard_map/middle/pallas_call | solution.py:358
  24.7 0.0 copy-start.6
  24.7 0.0 collective-permute-done.above
  24.7 9.0 %collective-permute-done.1.below = bf16[144,384]{1,0:T(8,128)(2,1)S(1)} collective-permute-done((bf16[144,384]{1,0:T(8,128)(2,1)}, bf16[144,384]{1,0:T(8,128)(2,1)S(1)}, u32[]{:S(2)}, u32[]{:S(2)}) %collective-permute-start.1) | collective-permute-done | bytes 110624 | tf_op jit(solution)/shard_map/ppermute | solution.py:356
  33.7 0.0 copy-done.1
  33.7 0.4 edge.1
  34.1 16.2 %all_to_all.25.parts = f32[32,4,384]{2,1,0:T(4,128)S(1)} all-to-all(f32[32,4,384]{2,1,0:T(4,128)S(1)} %get-tuple-element.33), channel_id=1, replica_groups={{0,4,8,12,16,20,24,28,32,36,40,44,48,52,56,60,64,68,72,76,80,84,88,92,9..., dimensions={0} | all-to-all | bytes 393216 | tf_op jit(solution)/shard_map/all_to_all | solution.py:35
  50.3 0.1 statistics.1
  50.4 20.3 %all_to_all.26.gathered = f32[16,4,384]{2,1,0:T(4,128)S(1)} all-to-all(f32[16,4,384]{2,1,0:T(4,128)S(1)} %statistics.1), channel_id=1, replica_groups={{0,1,2,3,128,129,130,131,256,257,258,259,384,385,386,387},{4,5,6,7,132,..., dimensions={0} | all-to-all | bytes 196608 | tf_op jit(solution)/shard_map/all_to_all | solution.py:35
  70.6 0.0 copy-done.3
  70.7 0.0 copy-done.10
  70.7 1.1 gradient.1
  71.7 1.7 %weights.1 = bf16[32,40,128]{2,1,0:T(8,128)(2,1)S(1)} custom-call(bf16[144,384]{1,0:T(8,128)(2,1)S(1)} %collective-permute-done.above, bf16[144,384]{1,0:T(8,128)(2,1)S(1)} %collective-permute-done.1.below, bf16[480,384]{1,0:T(8,128)(2,1)S(1)} %get-tuple-element.40.depth_mid, bf16[192,384]{1,0:T(8,128)(2,1)S(1)} %get-tuple-element.41.depth_edge, ...), custom_call_target="tpu_custom_call" | custom-call | bytes 1048576 | tf_op jit(solution)/shard_map/weights/pallas_call | solution.py:393
  73.4 14.8 %all_to_all.27.parts = bf16[32,40,128]{2,1,0:T(8,128)(2,1)S(1)} all-to-all(bf16[32,40,128]{2,1,0:T(8,128)(2,1)S(1)} %weights.1), channel_id=1, replica_groups={{0,4,8,12,16,20,24,28,32,36,40,44,48,52,56,60,64,68,72,76,80,84,88,92,9..., dimensions={0} | all-to-all | bytes 655360 | tf_op jit(solution)/shard_map/all_to_all | solution.py:35
  88.2 0.1 sum_plane.1
  88.3 16.1 %all_to_all.28.parts = bf16[16,40,128]{2,1,0:T(8,128)(2,1)S(1)} all-to-all(bf16[16,40,128]{2,1,0:T(8,128)(2,1)S(1)} %sum_plane.1), channel_id=1, replica_groups={{0,1,2,3,128,129,130,131,256,257,258,259,384,385,386,387},{4,5,6,7,132,..., dimensions={0} | all-to-all | bytes 327680 | tf_op jit(solution)/shard_map/all_to_all | solution.py:35
  104.4 0.8 sum_depth.1
  105.2 6.9 %all-to-all-start.4 = ((bf16[32,40,128]{2,1,0:T(8,128)(2,1)}), bf16[32,40,128]{2,1,0:T(8,128)(2,1)S(1)}, u32[]{:S(2)}, u32[]{:S(2)}) async-start(bf16[32,40,128]{2,1,0:T(8,128)(2,1)} %sum_depth.1), calls=%async_computation.4 | async-start | bytes 655360 | tf_op jit(solution)/shard_map/all_to_all | solution.py:35
  112.1 2.9 %levels.1 = (bf16[1,12,48,384]{3,2,1,0:T(8,128)(2,1)}, bf16[1,6,24,384]{3,2,1,0:T(8,128)(2,1)}) custom-call(f32[2]{0:T(128)} %mw.5, bf16[672,384]{1,0:T(8,128)(2,1)} %copy-done.4, f32[12,48,384]{2,1,0:T(8,128)} %copy-done.6, f32[3,3,384]{2,1,0:T(4,128)} %dw.5), custom_call_target="tpu_custom_call" | custom-call | flops 268435456 | bytes 1048576 | tf_op jit(solution)/shard_map/levels/pallas_call | solution.py:404
  115.0 6.7 %all-to-all-done.4.parts = bf16[32,40,128]{2,1,0:T(8,128)(2,1)S(1)} async-done(((bf16[32,40,128]{2,1,0:T(8,128)(2,1)}), bf16[32,40,128]{2,1,0:T(8,128)(2,1)S(1)}, u32[]{:S(2)}, u32[]{:S(2)}) %all-to-all-start.4) | async-done | bytes 327712 | tf_op jit(solution)/shard_map/all_to_all | solution.py:35
  121.7 0.8 finish.1
  (10 shorter events, 0.0 us)
Async XLA Ops:
  0.6 33.1 %copy-start.1 = (bf16[1,12,48,384]{3,2,1,0:T(8,128)(2,1)S(1)}, bf16[1,12,48,384]{3,2,1,0:T(8,128)(2,1)}, u32[]{:S(2)}) copy-start(bf16[1,12,48,384]{3,2,1,0:T(8,128)(2,1)} %cot.5) | copy-start | bytes 1327108
  4.9 19.9 %collective-permute-start = (bf16[144,384]{1,0:T(8,128)(2,1)}, bf16[144,384]{1,0:T(8,128)(2,1)S(1)}, u32[]{:S(2)}, u32[]{:S(2)}) collective-permute-start(bf16[144,384]{1,0:T(8,128)(2,1)} %get-tuple-element.28), channel_id=1, source_target_pairs={{0,1},{1,2},{2,3},{3,4},{4,5},{5,6},{6,7},{7,8},{8,9},{9,10},{10,1... | collective-permute-start | bytes 331784 | tf_op jit(solution)/shard_map/ppermute | solution.py:355
  14.5 19.2 %collective-permute-start.1 = (bf16[144,384]{1,0:T(8,128)(2,1)}, bf16[144,384]{1,0:T(8,128)(2,1)S(1)}, u32[]{:S(2)}, u32[]{:S(2)}) collective-permute-start(bf16[144,384]{1,0:T(8,128)(2,1)} %get-tuple-element.29), channel_id=1, source_target_pairs={{1,0},{2,1},{3,2},{4,3},{5,4},{6,5},{7,6},{8,7},{9,8},{10,9},{11,1... | collective-permute-start | bytes 331784 | tf_op jit(solution)/shard_map/ppermute | solution.py:356
  15.8 1.0 copy-start
  16.8 1.0 copy-start.2
  17.8 1.0 copy-start.5
  18.8 0.9 copy-start.7
  19.7 0.7 copy-start.8
  20.4 0.7 copy-start.9
  21.1 49.6 %copy-start.3 = (bf16[384,384]{1,0:T(8,128)(2,1)S(1)}, bf16[384,384]{1,0:T(8,128)(2,1)}, u32[]{:S(2)}) copy-start(bf16[384,384]{1,0:T(8,128)(2,1)} %pw.5) | copy-start | bytes 884740
  21.1 49.6 %copy-start.10 = (f32[384]{0:T(512)S(1)}, f32[384]{0:T(512)}, u32[]{:S(2)}) copy-start(f32[384]{0:T(512)} %gain.1) | copy-start | bytes 4612
  24.7 47.0 %copy-start.6 = (f32[12,48,384]{2,1,0:T(8,128)}, f32[12,48,384]{2,1,0:T(8,128)S(1)}, u32[]{:S(2)}) copy-start(f32[12,48,384]{2,1,0:T(8,128)S(1)} %get-tuple-element.37.slope) | copy-start | bytes 2654212
  71.7 1.7 %copy-start.4 = (bf16[672,384]{1,0:T(8,128)(2,1)}, bf16[672,384]{1,0:T(8,128)(2,1)S(1)}, u32[]{:S(2)}) copy-start(bf16[672,384]{1,0:T(8,128)(2,1)S(1)} %get-tuple-element.36.gmap) | copy-start | bytes 1548292
  105.2 16.5 %all-to-all-start.4 = ((bf16[32,40,128]{2,1,0:T(8,128)(2,1)}), bf16[32,40,128]{2,1,0:T(8,128)(2,1)S(1)}, u32[]{:S(2)}, u32[]{:S(2)}) async-start(bf16[32,40,128]{2,1,0:T(8,128)(2,1)} %sum_depth.1), calls=%async_computation.4 | async-start | bytes 655360 | tf_op jit(solution)/shard_map/all_to_all | solution.py:35
